TPU v7x, 32 devices: a whole 2x2x4 slice. The times are simulated.
32 devices in a mesh: dp: 8 (over y, x, core), seq: 4 (over z).
Axes of the slice: x: 2, y: 2, z: 4, core: 2. Of those that a mesh axis runs over, the one named last changes fastest.
Arguments:
- tokens: bfloat16 [16, 1024, 1536], P('dp', 'seq'), may hold values from -6 to 6
- lengths: int32 [16], P('dp'), may hold values from 1 to 1024, as said below
- in_weight: bfloat16 [1536, 6448], P(('dp', 'seq')), may hold values from -0.15625 to 0.15625
- conv_weight: bfloat16 [3328, 4], P(('dp', 'seq')), may hold values from -3 to 3
- conv_bias: bfloat16 [3328], P(('dp', 'seq')), may hold values from -1.5 to 1.5
- decay_log: float32 [48], replicated, may hold values from -6 to 1
- step_bias: float32 [48], replicated, may hold values from -4.5 to -2.5
- skip_gain: float32 [48], replicated, may hold values from 0.5 to 2
- norm_gain: bfloat16 [1536], P(('dp', 'seq')), may hold values from 0.5 to 1.5
- gate_gain: bfloat16 [3072], P(('dp', 'seq')), may hold values from 0.5 to 1.5
- out_weight: bfloat16 [3072, 1536], P(('dp', 'seq')), may hold values from -0.109375 to 0.109375
- cotangent: bfloat16 [16, 1024, 1536], P('dp', 'seq'), may hold values from -6 to 6
Outputs:
- output: bfloat16 [16, 1024, 1536], P('dp', 'seq')
- token_grad: bfloat16 [16, 1024, 1536], P('dp', 'seq')
- in_weight_grad: float32 [1536, 6448], P(('dp', 'seq'))
- conv_weight_grad: float32 [3328, 4], P(('dp', 'seq'))
- conv_bias_grad: float32 [3328], P(('dp', 'seq'))
- decay_log_grad: float32 [48], replicated
- step_bias_grad: float32 [48], replicated
- skip_gain_grad: float32 [48], replicated
- norm_gain_grad: float32 [1536], P(('dp', 'seq'))
- gate_gain_grad: float32 [3072], P(('dp', 'seq'))
- out_weight_grad: float32 [3072, 1536], P(('dp', 'seq'))
Inputs may be any that keep to these rules, and one draw needn't show every extreme that they name: `lengths`: among the 2 sequences of each dp index one, drawn from the seed, has length 1024.
All inputs are finite; a program needn't handle non-finite values.
Results may differ from a plain program's by a relative error of at most 0.0084.
Values may be sent and summed in bfloat16 or wider, within the bound.
A program may use at most 184 MiB of HBM per device.

v0:
```python
import jax
import jax.numpy as jnp
from jax import lax
from jax.sharding import PartitionSpec as P

D = 1536
DI = 3072
HEADS = 48
HDIM = 64
STATE = 128
CONV = 4
MICRO = 2
PROJ = 6448
CONV_CH = 3328


epsilon = 1e-05
highest = lax.Precision.HIGHEST


def from_behind(x, axis, by):
    devices = lax.axis_size(axis)
    pairs = [(i, i + by) for i in range(devices) if 0 <= i + by < devices]
    return lax.ppermute(x, axis, pairs)


def entering(x, axis, join, neutral):
    place = lax.axis_index(axis)
    gathered = jax.tree.map(
        lambda a, kind: lax.all_gather(a.astype(kind), axis), x, (jnp.bfloat16, jnp.bfloat16)
    )
    state = jax.tree.map(lambda a, e: jnp.zeros_like(a) + jnp.asarray(e, a.dtype), x, neutral)

    def one(hop, state):
        return join(
            state,
            jax.tree.map(
                lambda a, own: lax.dynamic_index_in_dim(a, hop, 0, False).astype(own.dtype),
                gathered,
                x,
            ),
        )

    return lax.fori_loop(0, place, one, state)


def entering_2(x, axis, combine, identity):
    devices, mine = (lax.axis_size(axis), lax.axis_index(axis))
    everything = jax.tree.map(lambda part: lax.all_gather(part, axis), x)
    start = jax.tree.map(
        lambda part, zero: jnp.broadcast_to(jnp.asarray(zero, part.dtype), part.shape), x, identity
    )

    def hop(k, before):
        at = devices - 1 - k
        reached = at > mine
        new = combine(before, jax.tree.map(lambda part: part[at], everything))
        return jax.tree.map(lambda a, b: jnp.where(reached, a, b), new, before)

    return lax.fori_loop(0, devices, hop, start)


def rms_scale(values):
    return lax.rsqrt(jnp.mean(values * values, axis=-1, keepdims=True) + epsilon)


def input_norm(inputs, gain):
    return inputs * rms_scale(inputs) * gain


def join_states(earlier, later):
    return (earlier[0] * later[0], later[0][:, :, None, None] * earlier[1] + later[1])


def conv_section(extended, step_raw, conv_weight, conv_bias, step_bias, decay_log):
    segment = extended.shape[1] - (CONV - 1)
    batch = extended.shape[0]
    mixed = conv_bias + jnp.zeros((batch, segment, extended.shape[2]), jnp.float32)
    for offset in range(CONV):
        mixed = mixed + conv_weight[:, offset] * extended[:, offset : offset + segment, :]
    active = jax.nn.silu(mixed)
    values_h = active[:, :, :DI].reshape(batch, segment, HEADS, HDIM)
    keys_b = active[:, :, DI : DI + STATE]
    reads_c = active[:, :, DI + STATE :]
    steps = jax.nn.softplus(step_raw + step_bias)
    log_decay = jnp.cumsum(steps * -jnp.exp(decay_log), axis=1)
    return (values_h, keys_b, reads_c, steps, log_decay)


def inner_block(values_h, keys_b, reads_c, steps, log_decay):
    count = log_decay.shape[0]
    causal = (jnp.arange(count)[:, None] >= jnp.arange(count)[None, :])[:, :, None]
    gaps = jnp.where(causal, log_decay[:, None, :] - log_decay[None, :, :], -1e30)
    fades = jnp.exp(gaps)
    intersection = jnp.dot(reads_c, keys_b.T, precision=highest)
    scaled = values_h * steps[:, :, None]
    return jnp.einsum("ijh,ij,jhp->ihp", fades, intersection, scaled, precision=highest)


def readout(values_h, keys_b, reads_c, steps, log_decay, skip_gain, state_in, gate_z, gate_gain):
    batch, segment = (values_h.shape[0], values_h.shape[1])
    inside = jax.vmap(inner_block)(values_h, keys_b, reads_c, steps, log_decay)
    carried = jnp.exp(log_decay)[:, :, :, None] * jnp.einsum(
        "shpn,sin->sihp", state_in, reads_c, precision=highest
    )
    mixed_y = inside + carried + skip_gain[None, None, :, None] * values_h
    gated = mixed_y.reshape(batch, segment, DI) * jax.nn.silu(gate_z)
    return gated * rms_scale(gated) * gate_gain


def carry_out(values_h, keys_b, steps, log_decay, state_in):
    tail_fade = jnp.exp(log_decay[:, -1:, :] - log_decay)
    local_part = jnp.einsum(
        "sjh,sjhp,sjn->shpn", tail_fade, values_h * steps[:, :, :, None], keys_b, precision=highest
    )
    return jnp.exp(log_decay[:, -1, :])[:, :, None, None] * state_in + local_part


def contract_rows(left, right):
    return lax.dot_general(
        left, right, (((0,), (0,)), ((), ())), preferred_element_type=jnp.float32
    )


def contract_cols(left, right):
    return lax.dot_general(
        left, right, (((1,), (1,)), ((), ())), preferred_element_type=jnp.float32
    )


def body(
    tokens,
    lengths,
    in_weight,
    conv_weight,
    conv_bias,
    decay_log,
    step_bias,
    skip_gain,
    norm_gain,
    gate_gain,
    out_weight,
    cotangent,
):
    seq_count, segment, width = tokens.shape
    per_batch = seq_count // MICRO
    rows = per_batch * segment
    channels = DI + 2 * STATE
    shards = (in_weight, conv_weight, conv_bias, norm_gain, gate_gain, out_weight)
    positions = lax.axis_index("seq") * segment + jnp.arange(segment)
    live_all = (positions[None, :] < lengths[:, None]).astype(jnp.float32)
    weight_totals = [
        jnp.zeros((D, PROJ), jnp.float32),
        jnp.zeros((CONV_CH, CONV), jnp.float32),
        jnp.zeros((CONV_CH,), jnp.float32),
        jnp.zeros((D,), jnp.float32),
        jnp.zeros((DI,), jnp.float32),
        jnp.zeros((DI, D), jnp.float32),
    ]
    head_totals = [
        jnp.zeros((HEADS,), jnp.float32),
        jnp.zeros((HEADS,), jnp.float32),
        jnp.zeros((HEADS,), jnp.float32),
    ]
    outputs = []
    input_grads = []
    for batch_index in range(MICRO):
        lower = batch_index * per_batch
        inputs = tokens[lower : lower + per_batch].astype(jnp.float32).reshape(rows, width)
        upstream = cotangent[lower : lower + per_batch].astype(jnp.float32).reshape(rows, width)
        live = live_all[lower : lower + per_batch].reshape(rows, 1)
        ahead = (
            lax.all_gather(shards[0], ("dp", "seq"), axis=0, tiled=True),
            lax.all_gather(shards[1], ("dp", "seq"), axis=0, tiled=True),
            lax.all_gather(shards[2], ("dp", "seq"), axis=0, tiled=True),
            lax.all_gather(shards[3], ("dp", "seq"), axis=0, tiled=True),
            lax.all_gather(shards[4], ("dp", "seq"), axis=0, tiled=True),
            lax.all_gather(shards[5], ("dp", "seq"), axis=0, tiled=True),
        )
        normed = input_norm(inputs, ahead[3].astype(jnp.float32)).astype(jnp.bfloat16)
        projected = jnp.dot(normed, ahead[0], preferred_element_type=jnp.float32)
        gate_z = projected[:, :DI].reshape(per_batch, segment, DI)
        conv_in = (
            projected[:, DI : DI + channels]
            .astype(jnp.bfloat16)
            .reshape(per_batch, segment, channels)
        )
        step_raw = projected[:, DI + channels :].reshape(per_batch, segment, HEADS)
        before = from_behind(conv_in[:, segment - (CONV - 1) :, :], "seq", 1)
        extended = jnp.concatenate([before, conv_in], axis=1).astype(jnp.float32)
        values_h, keys_b, reads_c, steps, log_decay = conv_section(
            extended,
            step_raw,
            ahead[1].astype(jnp.float32),
            ahead[2].astype(jnp.float32),
            step_bias,
            decay_log,
        )
        decay = jnp.exp(log_decay[:, -1, :])
        local_state = carry_out(
            values_h,
            keys_b,
            steps,
            log_decay,
            jnp.zeros((per_batch, HEADS, HDIM, STATE), jnp.float32),
        )
        prefix, state_in = entering(
            (decay, local_state),
            "seq",
            join_states,
            (jnp.ones_like(decay), jnp.zeros_like(local_state)),
        )
        normed_y = (
            readout(
                values_h,
                keys_b,
                reads_c,
                steps,
                log_decay,
                skip_gain,
                state_in,
                gate_z,
                ahead[4].astype(jnp.float32),
            )
            .reshape(rows, DI)
            .astype(jnp.bfloat16)
        )
        branch = jnp.dot(normed_y, ahead[5], preferred_element_type=jnp.float32)
        outputs.append(
            (inputs + live * branch).astype(jnp.bfloat16).reshape(per_batch, segment, width)
        )
        behind = (
            lax.all_gather(shards[0], ("dp", "seq"), axis=0, tiled=True),
            lax.all_gather(shards[1], ("dp", "seq"), axis=0, tiled=True),
            lax.all_gather(shards[2], ("dp", "seq"), axis=0, tiled=True),
            lax.all_gather(shards[3], ("dp", "seq"), axis=0, tiled=True),
            lax.all_gather(shards[4], ("dp", "seq"), axis=0, tiled=True),
            lax.all_gather(shards[5], ("dp", "seq"), axis=0, tiled=True),
        )
        masked = (live * upstream).astype(jnp.bfloat16)
        weight_totals[5] = weight_totals[5] + contract_rows(normed_y, masked)
        normed_y_grad = contract_cols(masked, behind[5]).reshape(per_batch, segment, DI)
        section_out, conv_pull = jax.vjp(
            conv_section,
            extended,
            step_raw,
            behind[1].astype(jnp.float32),
            behind[2].astype(jnp.float32),
            step_bias,
            decay_log,
        )
        values_h, keys_b, reads_c, steps, log_decay = section_out
        unused_y, read_pull = jax.vjp(
            readout,
            values_h,
            keys_b,
            reads_c,
            steps,
            log_decay,
            skip_gain,
            state_in,
            gate_z,
            behind[4].astype(jnp.float32),
        )
        read_grads = read_pull(normed_y_grad)
        later_prefix, later_grad = entering_2(
            (decay, read_grads[6]),
            "seq",
            join_states,
            (jnp.ones_like(decay), jnp.zeros_like(read_grads[6])),
        )
        unused_state, carry_pull = jax.vjp(carry_out, values_h, keys_b, steps, log_decay, state_in)
        carry_grads = carry_pull(later_grad)
        section_grads = (
            read_grads[0] + carry_grads[0],
            read_grads[1] + carry_grads[1],
            read_grads[2],
            read_grads[3] + carry_grads[2],
            read_grads[4] + carry_grads[3],
        )
        ext_grad, raw_grad, conv_w_grad, conv_b_grad, bias_grad, log_grad = conv_pull(section_grads)
        returned = from_behind(ext_grad[:, : CONV - 1, :].astype(jnp.bfloat16), "seq", -1).astype(
            jnp.float32
        )
        conv_grad = ext_grad[:, CONV - 1 :, :]
        conv_grad = conv_grad.at[:, segment - (CONV - 1) :, :].add(returned)
        projected_grad = (
            jnp.concatenate([read_grads[7], conv_grad, raw_grad], axis=2)
            .reshape(rows, PROJ)
            .astype(jnp.bfloat16)
        )
        weight_totals[0] = weight_totals[0] + contract_rows(normed, projected_grad)
        normed_grad = contract_cols(projected_grad, behind[0])
        unused_norm, norm_pull = jax.vjp(input_norm, inputs, behind[3].astype(jnp.float32))
        inputs_grad, gain_grad = norm_pull(normed_grad)
        input_grads.append(
            (upstream + inputs_grad).astype(jnp.bfloat16).reshape(per_batch, segment, width)
        )
        weight_totals[1] = weight_totals[1] + conv_w_grad
        weight_totals[2] = weight_totals[2] + conv_b_grad
        weight_totals[3] = weight_totals[3] + gain_grad
        weight_totals[4] = weight_totals[4] + read_grads[8]
        head_totals[0] = head_totals[0] + log_grad
        head_totals[1] = head_totals[1] + bias_grad
        head_totals[2] = head_totals[2] + read_grads[5]
    owned = (
        lax.psum_scatter(weight_totals[0], ("dp", "seq"), scatter_dimension=0, tiled=True),
        lax.psum_scatter(weight_totals[1], ("dp", "seq"), scatter_dimension=0, tiled=True),
        lax.psum_scatter(weight_totals[2], ("dp", "seq"), scatter_dimension=0, tiled=True),
        lax.psum_scatter(weight_totals[3], ("dp", "seq"), scatter_dimension=0, tiled=True),
        lax.psum_scatter(weight_totals[4], ("dp", "seq"), scatter_dimension=0, tiled=True),
        lax.psum_scatter(weight_totals[5], ("dp", "seq"), scatter_dimension=0, tiled=True),
    )
    head_sums = lax.psum((head_totals[0], head_totals[1], head_totals[2]), ("dp", "seq"))
    output = jnp.concatenate(outputs, axis=0)
    token_grad = jnp.concatenate(input_grads, axis=0)
    return (
        output,
        token_grad,
        owned[0],
        owned[1],
        owned[2],
        head_sums[0],
        head_sums[1],
        head_sums[2],
        owned[3],
        owned[4],
        owned[5],
    )


def solution(mesh):
    placed = (
        P("dp", "seq", None),
        P("dp"),
        P(("dp", "seq"), None),
        P(("dp", "seq"), None),
        P(("dp", "seq")),
        P(),
        P(),
        P(),
        P(("dp", "seq")),
        P(("dp", "seq")),
        P(("dp", "seq"), None),
        P("dp", "seq", None),
    )
    return jax.shard_map(
        body,
        mesh=mesh,
        in_specs=placed,
        out_specs=(
            P("dp", "seq", None),
            P("dp", "seq", None),
            P(("dp", "seq"), None),
            P(("dp", "seq"), None),
            P(("dp", "seq")),
            P(),
            P(),
            P(),
            P(("dp", "seq")),
            P(("dp", "seq")),
            P(("dp", "seq"), None),
        ),
        check_vma=False,
    )
```

profile of v0, /device:TPU:24, one launch (start us, length us, event | category | flops | bytes accessed | tf_op | source)
XLA Modules:
  0.0 1617.2 jit_solution(5337148805889185809)
XLA Ops:
  10.5 40.0 %all-reduce.34 = (bf16[1536]{0:T(1024)(128)(2,1)S(1)}, bf16[3328]{0:T(1024)(128)(2,1)S(1)}, bf16[3072]{0:T(1024)(128)(2,1)}) all-reduce(bf16[1536]{0:T(1024)(128)(2,1)S(1)} %dynamic-update-slice.6, bf16[3328]{0:T(1024)(128)(2,1)S(1)} %dynamic-update-slice.7, ...), channel_id=1, replica_groups=mesh['dp'=8,'seq'=4] {'dp','seq'}, use_global_device_ids=true, to_apply=%add.26 | all-reduce | flops 7936 | bytes 31744
  50.5 63.6 %all-gather.4 = bf16[32,104,4]{1,2,0:T(4,128)(2,1)S(1)} all-gather(bf16[1,104,4]{1,2,0:T(4,128)(2,1)} %bitcast.869), channel_id=1, replica_groups=mesh['dp'=8,'seq'=4] {'dp','seq'}, dimensions={0}, use_global_device_ids=true | all-gather | bytes 27456 | tf_op jit(solution)/shard_map/all_gather | solution.py:174
  118.1 23.7 %all-gather.12.cloned.1.call-done = bf16[1536,6448]{1,0:T(8,128)(2,1)} async-done(((bf16[48,6448]{1,0:T(8,128)(2,1)}), bf16[1536,6448]{1,0:T(8,128)(2,1)}) %all-gather.12.cloned.1.call-update) | async-done | bytes 19808272 | tf_op jit(solution)/shard_map/all_gather | solution.py:173
  141.8 14.3 fusion.268
  156.2 14.7 fusion.266
  264.8 12.3 all_gather.80
  304.6 15.1 fusion.96
  323.9 16.1 fusion.98
  340.0 28.9 %all-gather.14.cloned.1.call-done = bf16[3072,1536]{1,0:T(8,128)(2,1)} async-done(((bf16[96,1536]{1,0:T(8,128)(2,1)}), bf16[3072,1536]{1,0:T(8,128)(2,1)}) %all-gather.14.cloned.1.call-update) | async-done | bytes 9437200 | tf_op jit(solution)/shard_map/all_gather | solution.py:178
  368.9 9.9 multiply_reduce_fusion.9
  379.4 52.5 %all-gather.18.cloned.1.call-done = bf16[192,64,128]{2,1,0:T(8,128)(2,1)} async-done(((bf16[48,64,128]{2,1,0:T(8,128)(2,1)}), bf16[192,64,128]{2,1,0:T(8,128)(2,1)}) %all-gather.18.cloned.1.call-update) | async-done | bytes 3145744 | tf_op jit(solution)/shard_map/all_gather | solution.py:30
  442.8 15.1 fusion.95
  462.1 16.3 %fusion.97 = f32[1,256,48,64]{1,3,2,0:T(8,128)} fusion(f32[256,48,64]{0,2,1:T(8,128)S(1)} %fusion.181, f32[1,256,48,64]{1,3,2,0:T(8,128)S(1)} %bitcast.799, f32[256,48]{0,1:T(8,128)S(1)} %copy-done.100, f32[48]{0:T(128)S(1)} %copy-done.130, f32[256,48,64]{0,2,1:T(8,128)S(1)} %bitcast.798, f32[256,48]{0,1:T(8,128)S(1)} %copy-done.65, ...), kind=kOutput, calls=%fused_computation.136 | convolution fusion | flops 2429288448 | bytes 13058240 | tf_op jit(solution)/shard_map/vmap(ijh,ij,jhp->ihp)/dot_general | solution.py:97
  478.4 14.4 bitcast_multiply_fusion.17
  506.6 12.7 all_gather.91
  534.7 15.5 fusion.128
  550.7 25.0 %fusion.29 = (f32[256,48]{0,1:T(8,128)}, f32[256,48]{0,1:T(8,128)}, f32[256,256]{1,0:T(8,128)}, f32[256,256]{1,0:T(8,128)}, f32[256,48]{0,1:T(8,128)S(1)}, /*index=5*/f32[256,48]{0,1:T(8,128)S(1)}) fusion(f32[256,48]{0,1:T(8,128)S(1)} %copy-done.54, f32[256,256]{1,0:T(8,128)} %fusion.308, pred[256,256]{1,0:T(8,128)(4,1)S(1)} %copy-done.60, ...), kind=kOutput, calls=%fused_computation.41 | convolution fusion | flops 2473148416 | bytes 20332544 | tf_op jit(solution)/shard_map/transpose(jvp(vmap(ijh,ij,jhp->ihp)))/dot_general | solution.py:97
  611.9 11.8 fusion.9
  632.1 12.8 while.60
  663.7 64.3 %all-gather.22.cloned.1.call-done = f32[192,64,128]{2,1,0:T(8,128)} async-done(((f32[48,64,128]{2,1,0:T(8,128)}), f32[192,64,128]{2,1,0:T(8,128)}) %all-gather.22.cloned.1.call-update) | async-done | bytes 6291472 | tf_op jit(solution)/shard_map/all_gather | solution.py:49
  727.9 9.9 while.61
  764.1 18.6 %fusion.107 = (f32[1,256,48,64]{1,3,2,0:T(8,128)}, f32[256,48]{0,1:T(8,128)}, f32[256,48]{0,1:T(8,128)}, f32[1,256,48,64]{1,3,2,0:T(8,128)}) fusion(f32[1,256,48,64]{1,3,2,0:T(8,128)} %bitcast.814, f32[48,64,256]{2,1,0:T(8,128)} %get-tuple-element.749, f32[256,48]{0,1:T(8,128)S(1)} %copy-done.41, f32[256,48]{0,1:T(8,128)S(1)} %copy.385, ...), kind=kOutput, calls=%fused_computation.160 | convolution fusion | flops 2437914624 | bytes 32129216 | tf_op jit(solution)/shard_map/transpose(jvp(vmap(ijh,ij,jhp->ihp)))/dot_general | solution.py:97
  848.1 10.4 scatter-add.9
  858.5 10.0 scatter-add.6
  869.8 11.1 fusion.73
  880.9 12.3 fusion.158
  893.9 12.3 convolution_add_fusion.1
  906.3 18.1 %fusion.78 = f32[1536,6448]{1,0:T(8,128)} fusion(bf16[256,48]{0,1:T(8,128)(2,1)S(1)} %bitcast.854, bf16[256,3328]{0,1:T(8,128)(2,1)} %bitcast.827, bf16[256,3072]{0,1:T(8,128)(2,1)} %get-tuple-element.694, f32[1536]{0:T(1024)S(1)} %copy-done.45, f32[256]{0:T(256)S(1)} %copy-done.105, bf16[2,256,1536]{2,1,0:T(8,128)(2,1)S(1)} %copy-done.20), kind=kOutput, calls=%fused_computation.114 | convolution fusion | flops 5082390528 | bytes 43713536 | tf_op jit(solution)/shard_map/dot_general | solution.py:120
  924.4 26.1 %convolution_add_fusion = f32[1536,6448]{1,0:T(8,128)} fusion(f32[1536,6448]{1,0:T(8,128)} %fusion.78, bf16[256,48]{0,1:T(8,128)(2,1)S(1)} %bitcast.853, bf16[256,3328]{0,1:T(8,128)(2,1)} %bitcast.828, bf16[256,3072]{0,1:T(8,128)(2,1)} %get-tuple-element.695, f32[256]{0:T(256)S(1)} %copy-done.86, f32[1536]{0:T(1024)S(1)} %copy-done.45, ...), kind=kOutput, calls=%fused_computation.10 | convolution fusion | flops 5092294656 | bytes 83330048 | tf_op jit(solution)/shard_map/dot_general | solution.py:120
  968.2 52.9 %all-reduce.37.cloned.1.call-done = (f32[3328,4]{0,1:T(4,128)}, f32[3328]{0:T(1024)}, f32[48]{0:T(128)}, f32[48]{0:T(128)}, f32[48]{0:T(128)}, /*index=5*/f32[1536]{0:T(1024)}, f32[3072]{0:T(1024)}) async-done(((f32[3328,4]{0,1:T(4,128)}, f32[3328]{0:T(1024)}, f32[48]{0:T(128)}, f32[48]{0:T(128)}, f32[48]{0:T(128)}, /*index=5*/f32[1536]{0:T(1024)}, f32[3072]{0:T(1024)}), (f32[3328,4]{0,1:T(4,128)}, ...) | async-done | bytes 85584
  1026.2 207.7 %reduce-scatter.6.cloned.1.call-done = f32[96,1536]{1,0:T(8,128)} async-done(((f32[3072,1536]{1,0:T(8,128)}), f32[96,1536]{1,0:T(8,128)}) %reduce-scatter.6.cloned.1.call-update) | async-done | bytes 589840 | tf_op jit(solution)/shard_map/reduce_scatter | solution.py:312
  1233.9 372.9 %reduce-scatter.4.cloned.1.call-done = f32[48,6448]{1,0:T(8,128)} async-done(((f32[1536,6448]{1,0:T(8,128)}), f32[48,6448]{1,0:T(8,128)}) %reduce-scatter.4.cloned.1.call-update) | async-done | bytes 1238032 | tf_op jit(solution)/shard_map/reduce_scatter | solution.py:307
  (549 shorter events, 394.8 us)
Async XLA Ops:
  7.2 134.7 %all-gather.12.cloned.1.call-start = ((), (), s32[]{:S(2)}) async-start(), calls=%async_computation.2 | async-start | bytes 20680704 | tf_op jit(solution)/shard_map/all_gather | solution.py:173
  7.9 286.1 %all-gather.16.cloned.1.call-start = ((), (), s32[]{:S(2)}) async-start(), calls=%async_computation.6 | async-start | bytes 3932160 | tf_op jit(solution)/shard_map/all_gather | solution.py:30
  50.5 105.6 %copy-start.44 = (f32[1536]{0:T(1024)}, f32[1536]{0:T(1024)S(1)}, u32[]{:S(2)}) copy-start(f32[1536]{0:T(1024)S(1)} %convert_element_type.219) | copy-start | bytes 18436
  115.6 86.8 %copy-start.78 = (f32[3328]{0:T(1024)}, f32[3328]{0:T(1024)S(1)}, u32[]{:S(2)}) copy-start(f32[3328]{0:T(1024)S(1)} %get-tuple-element.612) | copy-start | bytes 39940
  117.4 38.8 %copy-start.111 = (f32[256]{0:T(256)}, f32[256]{0:T(256)S(1)}, u32[]{:S(2)}) copy-start(f32[256]{0:T(256)S(1)} %get-tuple-element.607) | copy-start | bytes 3076
  118.0 52.9 %copy-start.121 = (f32[48]{0:T(128)}, f32[48]{0:T(128)S(1)}, u32[]{:S(2)}) copy-start(f32[48]{0:T(128)S(1)} %exponential_negate_fusion) | copy-start | bytes 580
  118.1 38.1 %copy-start.85 = (f32[256]{0:T(256)}, f32[256]{0:T(256)S(1)}, u32[]{:S(2)}) copy-start(f32[256]{0:T(256)S(1)} %fusion.351) | copy-start | bytes 3076
  118.1 38.1 %copy-start.104 = (f32[256]{0:T(256)}, f32[256]{0:T(256)S(1)}, u32[]{:S(2)}) copy-start(f32[256]{0:T(256)S(1)} %fusion.350) | copy-start | bytes 3076
  118.1 38.1 %copy-start.19 = (bf16[2,256,1536]{2,1,0:T(8,128)(2,1)S(1)}, bf16[2,256,1536]{2,1,0:T(8,128)(2,1)}, u32[]{:S(2)}) copy-start(bf16[2,256,1536]{2,1,0:T(8,128)(2,1)} %param.25) | copy-start | bytes 4718596
  184.4 9.1 collective-permute-start
  188.9 11.0 collective-permute-start.1
  213.9 76.5 %copy-start.12 = (f32[1,256,3328]{1,2,0:T(8,128)}, f32[1,256,3328]{1,2,0:T(8,128)S(1)}, u32[]{:S(2)}) copy-start(f32[1,256,3328]{1,2,0:T(8,128)S(1)} %get-tuple-element.730) | copy-start | bytes 10223620
  220.1 148.8 %all-gather.14.cloned.1.call-start = ((), (), s32[]{:S(2)}) async-start(), calls=%async_computation.3 | async-start | bytes 9732096 | tf_op jit(solution)/shard_map/all_gather | solution.py:178
  220.9 211.0 %all-gather.18.cloned.1.call-start = ((), (), s32[]{:S(2)}) async-start(), calls=%async_computation.7 | async-start | bytes 3932160 | tf_op jit(solution)/shard_map/all_gather | solution.py:30
  222.2 256.1 %copy-start.106 = (f32[1,256]{1,0:T(1,128)}, f32[1,256]{1,0:T(1,128)S(1)}, u32[]{:S(2)}) copy-start(f32[1,256]{1,0:T(1,128)S(1)} %get-tuple-element.740) | copy-start | bytes 3076
  227.0 59.9 %copy-start.35 = (f32[1,48,256]{1,2,0:T(8,128)}, f32[1,48,256]{1,2,0:T(8,128)S(1)}, u32[]{:S(2)}) copy-start(f32[1,48,256]{1,2,0:T(8,128)S(1)} %get-tuple-element.689) | copy-start | bytes 147460
  294.0 338.1 %all-gather.20.cloned.1.call-start = ((), (), s32[]{:S(2)}) async-start(), calls=%async_computation.8 | async-start | bytes 7864320 | tf_op jit(solution)/shard_map/all_gather | solution.py:49
  304.5 19.3 %copy-start.27 = (f32[256,48,64]{0,2,1:T(8,128)}, f32[256,48,64]{0,2,1:T(8,128)S(1)}, u32[]{:S(2)}) copy-start(f32[256,48,64]{0,2,1:T(8,128)S(1)} %fusion.185) | copy-start | bytes 9437188
  323.9 45.0 %copy-start.124 = (f32[256]{0:T(256)}, f32[256]{0:T(256)S(1)}, u32[]{:S(2)}) copy-start(f32[256]{0:T(256)S(1)} %fusion.352) | copy-start | bytes 3076
  323.9 45.0 %copy-start.30 = (bf16[2,256,1536]{2,1,0:T(8,128)(2,1)S(1)}, bf16[2,256,1536]{2,1,0:T(8,128)(2,1)}, u32[]{:S(2)}) copy-start(bf16[2,256,1536]{2,1,0:T(8,128)(2,1)} %param.36) | copy-start | bytes 4718596
  323.9 45.0 %copy-start.108 = (f32[1,256]{1,0:T(1,128)S(1)}, f32[1,256]{1,0:T(1,128)}, u32[]{:S(2)}) copy-start(f32[1,256]{1,0:T(1,128)} %get-tuple-element.739) | copy-start | bytes 3076
  442.7 19.3 %copy-start.28 = (f32[256,48,64]{0,2,1:T(8,128)}, f32[256,48,64]{0,2,1:T(8,128)S(1)}, u32[]{:S(2)}) copy-start(f32[256,48,64]{0,2,1:T(8,128)S(1)} %fusion.181) | copy-start | bytes 9437188
  457.9 20.5 %copy-start.17 = (f32[1,256,48,64]{1,3,2,0:T(8,128)}, f32[1,256,48,64]{1,3,2,0:T(8,128)S(1)}, u32[]{:S(2)}) copy-start(f32[1,256,48,64]{1,3,2,0:T(8,128)S(1)} %fusion.95) | copy-start | bytes 9437188
  499.2 228.7 %all-gather.22.cloned.1.call-start = ((), (), s32[]{:S(2)}) async-start(), calls=%async_computation.9 | async-start | bytes 7864320 | tf_op jit(solution)/shard_map/all_gather | solution.py:49
  550.2 470.8 %all-reduce.37.cloned.1.call-start = ((), (), s32[]{:S(2)}) async-start(), calls=%async_computation.10 | async-start | bytes 183296
  647.9 80.0 %copy-start.5 = (f32[1,48,64,128]{3,2,1,0:T(8,128)S(1)}, f32[1,48,64,128]{3,2,1,0:T(8,128)}, u32[]{:S(2)}) copy-start(f32[1,48,64,128]{3,2,1,0:T(8,128)} %custom-call.1) | copy-start | bytes 4718596
  662.6 65.3 %copy-start.56 = (f32[1,48,2,128]{3,1,2,0:T(8,128)}, f32[1,48,2,128]{3,1,2,0:T(8,128)S(1)}, u32[]{:S(2)}) copy-start(f32[1,48,2,128]{3,1,2,0:T(8,128)S(1)} %reduce-window.50) | copy-start | bytes 147460
  819.3 22.2 %collective-permute-start.3 = (bf16[1,3,3328]{2,1,0:T(4,128)(2,1)}, bf16[1,3,3328]{2,1,0:T(4,128)(2,1)}, u32[]{:S(2)}, u32[]{:S(2)}) collective-permute-start(bf16[1,3,3328]{2,1,0:T(4,128)(2,1)} %copy.409), channel_id=1, source_target_pairs={{1,0},{2,1},{3,2},{5,4},{6,5},{7,6},{9,8},{10,9},{11,10},{13,12},{... | collective-permute-start | bytes 59912 | tf_op jit(solution)/shard_map/ppermute | solution.py:24
  839.0 6.1 collective-permute-start.2
  848.1 21.7 %copy-start.34 = (bf16[256,3072]{0,1:T(8,128)(2,1)S(1)}, bf16[256,3072]{0,1:T(8,128)(2,1)}, u32[]{:S(2)}) copy-start(bf16[256,3072]{0,1:T(8,128)(2,1)} %get-tuple-element.695) | copy-start | bytes 4718596
  893.8 340.1 %reduce-scatter.6.cloned.1.call-start = ((), (), s32[]{:S(2)}) async-start(), calls=%async_computation.5 | async-start | bytes 19464192 | tf_op jit(solution)/shard_map/reduce_scatter | solution.py:312
  906.2 700.6 %reduce-scatter.4.cloned.1.call-start = ((), (), s32[]{:S(2)}) async-start(), calls=%async_computation.4 | async-start | bytes 41361408 | tf_op jit(solution)/shard_map/reduce_scatter | solution.py:307
  (123 other events, 879.6 us)
Sparse Core Ops, SparseCore 0:
  10.8 130.9 all-gather.11
  220.3 63.9 all-gather.15
  287.1 81.8 all-gather.13
  370.9 60.9 all-gather.17
  499.3 113.4 all-gather.19
  614.3 113.5 all-gather.21
  894.0 127.0 all-reduce.36
  1029.1 204.7 reduce-scatter.5
  1242.1 364.7 reduce-scatter.3
where the time goes:
time: 1630 us; the launch traced here: 1620 us
  waiting for transfers between devices  804 us (49%)
  matrix products  355 us (22%)
  other arithmetic  169 us (10%)
  blocking collectives  145 us (9%)
  local copies, waits for them, and re-layouts  117 us (7%)
  between operations  16.3 us (1%)
    reduce_scatter x1, waiting for transfers between devices, body(): lax.psum_scatter(weight_totals[0], ('dp', 'seq'), scatter_dimension=0, ti...  373 us
    reduce_scatter x1, waiting for transfers between devices, body(): lax.psum_scatter(weight_totals[5], ('dp', 'seq'), scatter_dimension=0, ti...  208 us
    dot_general x8, matrix products, inner_block(): jnp.einsum('ijh,ij,jhp->ihp', fades, intersection, scaled, precision=high...  133 us
    dot_general x4, matrix products, contract_rows(): lax.dot_general(left, right, (((0,), (0,)), ((), ())), preferred_element_...  64.9 us
    all_gather x2, waiting for transfers between devices, entering_2(): everything = jax.tree.map(lambda part: lax.all_gather(part, axis), x)  64.3 us
    all_gather x1, blocking collectives, body(): lax.all_gather(shards[1], ('dp', 'seq'), axis=0, tiled=True)  63.6 us
    unnamed x10, waiting for transfers between devices  54.3 us
    all_gather x2, waiting for transfers between devices, entering(): lax.all_gather(a.astype(kind), axis)  52.5 us
  transfers between devices with their start and end apart: 13, of which 7 were waited for; matrix products, arithmetic and copies ran while one was open for 23% of the time, Pallas kernels for 0%

commit v1 on v0

v1 whole, which is shorter than its diff:
```python
import functools
import jax
import jax.numpy as jnp
from jax import lax
from jax.experimental import pallas as pl
from jax.experimental.pallas import tpu as pltpu
from jax.sharding import PartitionSpec as P

D = 1536
DI = 3072
HEADS = 48
HDIM = 64
STATE = 128
CONV = 4
PROJ = 6448
CONV_CH = 3328
CW = 384
GROUPS = DI // CW
GH = CW // HDIM
NI = 1 + 2 * GROUPS
NO = D // CW
MID = 2 + GROUPS
GATE = MID + NO // 2
LATE = GATE + GROUPS
HALO = 16
EPS = 1e-05
MESH = pl.DeviceIdType.MESH
HIGH = lax.Precision.HIGHEST
f32 = jnp.float32
bf16 = jnp.bfloat16
AXES = ("dp", "seq")
LAG = 2
AHEAD = 4


def flip(p, w):
    return p + w * (1 - 2 * lax.rem(lax.div(p, w), 2))


class Place:
    def __init__(self, S, PL):
        self.S, self.PL, self.m = S, PL, PL.bit_length() - 1
        self.d = lax.axis_index("dp")
        self.z = lax.axis_index("seq")
        self.p = lax.div(self.d, 2)
        self.c = lax.rem(self.d, 2)
        self.sib = self.d + 1 - 2 * self.c

    def weight(self, j, h):
        return 2 ** ((j + h) % self.m)

    def held(self, h, j):
        out = [self.p]
        for i in range(j):
            out = out + [flip(q, self.weight(i, h)) for q in out]
        return out

    def across(self, j, h):
        return (2 * flip(self.p, self.weight(j, h)) + self.c, self.z)

    def along(self, o):
        return (self.d, lax.rem(self.z + o, self.S))

    def behind(self, o):
        return lax.rem(self.z - o + self.S, self.S)

    def barrier(self):
        peers = [self.along(o) for o in range(1, self.S)]
        peers += [self.across(j, 0) for j in range(self.m)]
        peers += [(self.sib, self.z)]
        bar = pltpu.get_barrier_semaphore()
        for q in peers:
            pl.semaphore_signal(bar, inc=1, device_id=q, device_id_type=MESH)
        pl.semaphore_wait(bar, len(peers))


def remote(src, dst, ss, rs, to):
    return pltpu.make_async_remote_copy(
        src_ref=src, dst_ref=dst, send_sem=ss, recv_sem=rs, device_id=to, device_id_type=MESH
    )


def picks(rows, R, padded):
    i = lax.broadcasted_iota(jnp.int32, (rows, rows // R * padded), 0)
    j = lax.broadcasted_iota(jnp.int32, (rows, rows // R * padded), 1)
    out = jnp.zeros(i.shape, jnp.bool_)
    for b in range(rows // R):
        inside = (i >= b * R) & (i < b * R + R)
        out = out | (inside & (j - b * padded == i - b * R))
    return jnp.where(out, 1.0, 0.0).astype(bf16)


class Gather:
    def __init__(self, at, sems, arrays):
        self.at = at
        self.zs, self.zr, self.xs, self.xr, self.cs, self.cr = sems
        self.arrays = arrays

    def each(self, k, f):
        for among, fn, land, R in self.arrays:
            if isinstance(k, int):
                if among(k):
                    f(fn(k), R, land and land(k))
            else:
                @pl.when(among(k))
                def _():
                    f(fn(k), R, land and land(k))

    def zcopy(self, ref, R, land, k, o, recv=False):
        at = self.at
        src = at.behind(o) if recv else at.z
        blk = ref.at[pl.ds((at.d * at.S + src) * R, R)] if land is None else land.at[src]
        return remote(blk, blk, self.zs.at[k, o - 1], self.zr.at[k, o - 1], at.along(o))

    def half(self, ref, R, q, c, h):
        n = self.at.S * R // 2
        return ref.at[pl.ds((q * 2 + c) * self.at.S * R + h * n, n)]

    def xcopy(self, ref, R, k, j, i, h, recv=False):
        at = self.at
        q = at.held(h, j)[i]
        if recv:
            q = flip(q, at.weight(j, h))
        blk = self.half(ref, R, q, at.c, h)
        n = (2**j - 1 + i) * 2 + h
        return remote(blk, blk, self.xs.at[k, n], self.xr.at[k, n], at.across(j, h))

    def ccopy(self, ref, R, k, n, h, recv=False):
        at = self.at
        q = at.held(h, at.m)[n]
        blk = self.half(ref, R, q, 1 - at.c if recv else at.c, h)
        return remote(blk, blk, self.cs.at[k, n * 2 + h], self.cr.at[k, n * 2 + h], (at.sib, at.z))

    def send_z(self, k):
        def f(ref, R, land):
            for o in range(1, self.at.S):
                self.zcopy(ref, R, land, k, o).start()

        self.each(k, f)

    def stage(self, k, j):
        def f(ref, R, land):
            if j == 0:
                for o in range(1, self.at.S):
                    self.zcopy(ref, R, land, k, o, True).wait_recv()
                if land is not None:
                    rows = self.at.S * R
                    own = ref.at[pl.ds(pl.multiple_of(self.at.d * rows, 16), rows)]
                    own[...] = dot(picks(rows, R, land.shape[1]), land[...].reshape(-1, land.shape[2])).astype(bf16)
            else:
                for h in range(2):
                    for i in range(2 ** (j - 1)):
                        self.xcopy(ref, R, k, j - 1, i, h, True).wait_recv()
            if j < self.at.m:
                for h in range(2):
                    for i in range(2**j):
                        self.xcopy(ref, R, k, j, i, h).start()
            for h in range(2):
                for n in range(0 if j == 0 else 2 ** (j - 1), 2**j):
                    self.ccopy(ref, R, k, n, h).start()

        self.each(k, f)

    def arrived(self, k):
        def f(ref, R, land):
            for n in range(self.at.PL):
                for h in range(2):
                    self.ccopy(ref, R, k, n, h, True).wait_recv()

        self.each(k, f)

    def sent(self, k):
        def f(ref, R, land):
            for o in range(1, self.at.S):
                self.zcopy(ref, R, land, k, o).wait_send()
            for h in range(2):
                for j in range(self.at.m):
                    for i in range(2**j):
                        self.xcopy(ref, R, k, j, i, h).wait_send()
                for n in range(self.at.PL):
                    self.ccopy(ref, R, k, n, h).wait_send()

        self.each(k, f)


def lanes128(r):
    return jnp.concatenate([r, jnp.zeros((r.shape[0], 128 - r.shape[1]), r.dtype)], axis=1)


def set_heads(heads, decay, bias, skips):
    rows = [bias[...], -jnp.exp(decay[...]), skips[...]]
    heads[...] = jnp.concatenate([lanes128(r) for r in rows] + [jnp.zeros((5, 128), f32)], axis=0)


def sigmoid(v):
    return 1.0 / (1.0 + jnp.exp(-v))


NT = ((1,), (1,))
TN = ((0,), (0,))


def dot(a, b, dims=((1,), (0,)), precision=None):
    return lax.dot_general(a, b, (dims, ((), ())), precision=precision, preferred_element_type=f32)


def halves(v):
    hi = v.astype(bf16)
    return hi, (v - hi.astype(f32)).astype(bf16)


def spread(cols, g6):
    T = cols.shape[0]
    low = lax.broadcasted_iota(jnp.int32, (T, 128), 1) < HDIM
    return jnp.concatenate(
        [
            jnp.where(
                low,
                jnp.broadcast_to(cols[:, 2 * q : 2 * q + 1], (T, 128)),
                jnp.broadcast_to(cols[:, 2 * q + 1 : 2 * q + 2], (T, 128)),
            )
            for q in range(GH // 2)
        ],
        axis=1,
    )


def turned(x, g):
    return pltpu.roll(x, lax.rem(128 - GH * g, 128), 1)


def convolve(x, cp):
    T = x.shape[0] - HALO
    mixed = cp[4:5] + cp[3:4] * x[HALO:]
    for k in range(CONV - 1):
        mixed = mixed + cp[k : k + 1] * pltpu.roll(x, CONV - 1 - k, 0)[HALO:]
    return mixed


def columns(count, first):
    ch = (lax.broadcasted_iota(jnp.int32, (1, CW), 1) + first).astype(f32)
    place = ch - count * jnp.floor((ch + 0.5) / count)
    return jnp.where(lax.broadcasted_iota(jnp.int32, (128, CW), 0).astype(f32) == place, 1.0, 0.0)


def prepare(s, raw, x, heads, cp, ld, ldT, gram):
    T = raw.shape[0]
    steps = jax.nn.softplus(raw + heads[0:1])
    tri = lax.broadcasted_iota(jnp.int32, (T, T), 0) >= lax.broadcasted_iota(jnp.int32, (T, T), 1)
    log_decay = dot(jnp.where(tri, 1.0, 0.0), steps * heads[1:2], precision=HIGH)
    ld[0, s] = log_decay
    ld[1, s] = steps
    turned_ld = log_decay.T
    for g in range(GROUPS):
        ldT[s, g, 0:GH] = turned_ld[g * GH : (g + 1) * GH]
    mixed = convolve(x, cp)[:, : 2 * STATE]
    act = mixed * sigmoid(mixed)
    keys, reads = act[:, :STATE], act[:, STATE:]
    gram[s] = dot(reads, keys, ((1,), (1,)), HIGH)
    return keys, reads, mixed


def fade(ldc, ldr, h, lo, n, m):
    gap = ldc[lo : lo + n, h : h + 1] - ldr[h : h + 1, :m]
    i = lax.broadcasted_iota(jnp.int32, (n, m), 0) + lo
    j = lax.broadcasted_iota(jnp.int32, (n, m), 1)
    return jnp.exp(jnp.where(i >= j, gap, -1e30))


def forward_kernel(S, PL, lengths, tok, win, cw, cb, ng_in, gg_in, decay, bias, skips, wout, cot,
                   out, owin, onormed, opc, oraw, oz, oy, ohin, ony, oconv, ogain, ossq, ong, odny, otsum, old, oldT, ogram, okeys2, oreadsT,
                   wi, wo, sm, zi, zo, halo, normed, ybuf, nyb, loc, hin, hout, dlast, gram, keysT, reads2, keys2, readsT,
                   ld, ldT, convp, gain, ngain, ssq, tsum, heads, pcs, zst, yst,
                   lsem, osem, hsem, ssem, pcsem, zsem, ysem, esem, nsem, cotsem, *sems):
    at = Place(S, PL)
    me = at.d * S + at.z
    seqs, T, _ = tok.shape
    rows = seqs * T
    n = 1 + NI + NO
    nd = S * PL * 2
    RI, RO = D // nd, DI // nd
    packed_i, packed_o = RI % 16 > 0, RO % 16 > 0

    def in_i(k):
        return (k >= 1) & (k < LATE) & ((k < MID) | (k >= GATE))

    def in_o(k):
        return ((k >= MID) & (k < GATE)) | ((k >= LATE) & (k < n))

    def chunk_i(k):
        return k - 1 - (NO // 2) * lax.div(k, GATE)

    def chunk_o(k):
        return k - MID - GROUPS * lax.div(k, LATE)

    ga = Gather(at, sems, [
        (lambda k: k == 0, lambda k: sm, None, 16),
        (in_i, lambda k: wi.at[chunk_i(k)], (lambda k: zi.at[chunk_i(k)]) if packed_i else None, RI),
        (in_o, lambda k: wo.at[chunk_o(k)], (lambda k: zo.at[chunk_o(k)]) if packed_o else None, RO),
    ])

    def local(c):
        return pltpu.make_async_copy(
            wout.at[:, pl.ds(c * CW, CW)], zo.at[c, at.z] if packed_o else wo.at[c, pl.ds(me * RO, RO)], lsem.at[c])

    for c in range(NO):
        local(c).start()
    for j in range(NI):
        lane = 2 * DI if j == 0 else DI + (j - 1) * CW if j <= GROUPS else (j - 1 - GROUPS) * CW
        part = win[:, lane:] if j == 0 else win[:, lane : lane + CW]
        if j == 0:
            part = jnp.concatenate([part, jnp.zeros((part.shape[0], CW - part.shape[1]), bf16)], axis=1)
        if packed_i:
            zi[j, at.z] = part
        else:
            wi[j, pl.ds(pl.multiple_of(me * RI, 16), RI)] = part
    own = [lanes128(r[...].astype(f32)) for r in (cw, cb, ng_in, gg_in)] + [jnp.zeros((9, 128), f32)]
    sm[pl.ds(pl.multiple_of(me * 16, 16), 16)] = jnp.concatenate(own, axis=0).astype(bf16)
    set_heads(heads, decay, bias, skips)
    at.barrier()
    for c in range(NO):
        local(c).wait()
    for k in range(AHEAD):
        ga.send_z(k)

    def halo_copy():
        return remote(tok.at[:, pl.ds(T - HALO, HALO)], halo, hsem.at[0], hsem.at[1], at.along(1))

    @pl.when(at.z < S - 1)
    def _():
        halo_copy().start()

    @pl.when(at.z == 0)
    def _():
        halo[...] = jnp.zeros_like(halo)
        hin[...] = jnp.zeros_like(hin)

    @pl.when(at.z > 0)
    def _():
        halo_copy().wait_recv()

    ssq[...] = jnp.zeros_like(ssq)

    def chain(g):
        return remote(hout.at[g], hin.at[g], ssem.at[0, g], ssem.at[1, g], at.along(1))

    def normed_copies():
        return [pltpu.make_async_copy(normed.at[s, pl.ds(HALO, T), pl.ds(c * CW, CW)],
                                      onormed.at[c, pl.ds(s * T, T)], nsem.at[c, s])
                for c in range(D // CW) for s in range(seqs)]

    def unpack():
        gathered = sm[...]

        def rows_of(count, first):
            wide = dot(gathered, columns(count, first).astype(bf16)).reshape(nd, 16, CW)
            who = lax.broadcasted_iota(jnp.int32, (nd, 1, CW), 0) * count
            at_lane = lax.broadcasted_iota(jnp.int32, (nd, 1, CW), 2) + first
            wide = jnp.where((at_lane >= who) & (at_lane < who + count), wide, 0.0)
            return jnp.sum(wide, axis=0)[:8]

        def group(g, carry):
            convp[1 + g] = rows_of(CONV_CH // nd, g * CW)
            gain[g] = rows_of(DI // nd, g * CW)
            return carry

        lax.fori_loop(0, GROUPS, group, 0)
        convp[0] = rows_of(CONV_CH // nd, DI)
        ng = jnp.concatenate([rows_of(D // nd, g * CW)[5:6] for g in range(D // CW)], axis=1)
        ngain[...] = jnp.broadcast_to(ng, (8, D))
        pltpu.make_async_copy(ngain, ong, esem.at[4 + seqs]).start()
        for s in range(seqs):
            u = halo[s].astype(f32)
            r = lax.rsqrt(jnp.sum(u * u, axis=1, keepdims=True) * (1.0 / D) + EPS)
            normed[s, 0:HALO] = (u * r * ng).astype(bf16)
            for i in range(0, T, 64):
                u = tok[s, i : i + 64].astype(f32)
                r = lax.rsqrt(jnp.sum(u * u, axis=1, keepdims=True) * (1.0 / D) + EPS)
                normed[s, HALO + i : HALO + i + 64] = (u * r * ng).astype(bf16)
        for c in normed_copies():
            c.start()
        pltpu.make_async_copy(convp, oconv, esem.at[2 + seqs]).start()
        pltpu.make_async_copy(gain, ogain, esem.at[3 + seqs]).start()

    def project(w, first):
        x = normed[...] if first == 0 else normed[:, first:]
        return dot(x.reshape(seqs * x.shape[1], D), w).reshape(seqs, x.shape[1], CW)

    def keep_pc(pc, k, slot):
        pcs[slot] = pc
        pltpu.make_async_copy(pcs.at[slot], opc.at[k], pcsem.at[slot]).start()

    def prepared():
        pairs = ((ld, old), (ldT, oldT), (gram, ogram), (keys2, okeys2), (readsT, oreadsT))
        return [pltpu.make_async_copy(a, b, esem.at[seqs + 6 + i]) for i, (a, b) in enumerate(pairs)]

    def first_chunk():
        proj = project(wi[0], 0)
        pc = proj.astype(bf16)
        keep_pc(pc, 0, 0)
        raw = proj[:, HALO:, 2 * STATE :]
        zst[0, :, :, :128] = raw
        pltpu.make_async_copy(zst.at[0, :, :, pl.ds(0, 128)], oraw, zsem.at[0]).start()
        for s in range(seqs):
            keys, reads = prepare(s, raw[s], pc[s].astype(f32), heads, convp[0], ld, ldT, gram)[:2]
            keysT[s] = keys.T
            readsT[s] = reads.T
            reads2[s] = jnp.concatenate(halves(reads), axis=1)
            keys2[s] = jnp.concatenate(halves(keys), axis=1)
        for c in prepared():
            c.start()
        pltpu.make_async_copy(zst.at[0, :, :, pl.ds(0, 128)], oraw, zsem.at[0]).wait()

    def values_chunk(g, k):
        slot = lax.rem(k, 2)

        @pl.when(k >= 2)
        def _():
            pltpu.make_async_copy(pcs.at[slot], opc.at[k - 2], pcsem.at[slot]).wait()

        pc = project(wi[k], 0).astype(bf16)
        keep_pc(pc, k, slot)
        cp = convp[k]
        low = lax.broadcasted_iota(jnp.int32, (T // 2, 128), 1) < HDIM
        skip = spread(turned(jnp.broadcast_to(heads[2:3], (8, 128)), g), 0)[0:1]

        def sequence(s, carry):
            mixed = convolve(pcs[slot, s].astype(f32), cp)
            V = mixed * sigmoid(mixed)
            ldc = turned(ld[0, s], g)
            ldr = ldT[s, g]
            X = V * spread(turned(ld[1, s], g), g)
            lde = spread(ldc, g)
            last = lde[T - 1 : T]
            dlast[g, s] = jnp.broadcast_to(jnp.exp(last), (8, CW))
            loc[g, s] = dot(keysT[s], X * jnp.exp(last - lde), precision=HIGH)
            hi, lo = halves(X)
            H = T // 2
            for q in range(GH // 2):
                sl = slice(q * 128, q * 128 + 128)
                xs = jnp.concatenate([hi[:, sl], lo[:, sl]], axis=1)
                top, bot = [], []
                for h in (2 * q, 2 * q + 1):
                    mt = (gram[s, :H, :H] * fade(ldc, ldr, h, 0, H, H)).astype(bf16)
                    mb = (gram[s, H:, :] * fade(ldc, ldr, h, H, H, T)).astype(bf16)
                    r = dot(mt, xs[:H])
                    top.append(r[:, :128] + r[:, 128:])
                    r = dot(mb, xs)
                    bot.append(r[:, :128] + r[:, 128:])
                ybuf[g, s, :H, sl] = jnp.where(low, top[0], top[1]) + skip[:, sl] * V[:H, sl]
                ybuf[g, s, H:, sl] = jnp.where(low, bot[0], bot[1]) + skip[:, sl] * V[H:, sl]
            return carry

        lax.fori_loop(0, seqs, sequence, 0)

    def pass_state(g):
        @pl.when(at.z > 0)
        def _():
            chain(g).wait_recv()

        @pl.when(at.z < S - 1)
        def _():
            for s in range(seqs):
                hout[g, s] = (dlast[g, s, 0:1] * hin[g, s].astype(f32) + loc[g, s]).astype(bf16)
            chain(g).start()

    def y_copy(i):
        a = lax.rem(i, 2)
        return pltpu.make_async_copy(yst.at[a], oy.at[lax.div(i, seqs), lax.rem(i, seqs)], ysem.at[a])

    def gate_chunk(g, k):
        slot = lax.rem(g, 2)

        @pl.when(g >= 2)
        def _():
            pltpu.make_async_copy(zst.at[slot], oz.at[g - 2], zsem.at[slot]).wait()

        zst[slot] = project(wi[k], HALO)
        pltpu.make_async_copy(zst.at[slot], oz.at[g], zsem.at[slot]).start()

        def sequence(s, carry):
            z = zst[slot, s]
            h2 = jnp.concatenate([hin[g, s], hin[g, s]], axis=0)
            carried = dot(reads2[s], h2) * jnp.exp(spread(turned(ld[0, s], g), g))
            y = ybuf[g, s] + carried
            i = g * seqs + s

            @pl.when(i >= 2)
            def _():
                y_copy(i - 2).wait()

            yst[lax.rem(i, 2)] = y
            y_copy(i).start()
            gated = y * (z * sigmoid(z))
            ybuf[g, s] = gated
            ssq[s] += jnp.broadcast_to(jnp.sum(gated * gated, axis=1, keepdims=True), (T, 128))
            return carry

        lax.fori_loop(0, seqs, sequence, 0)

        @pl.when(g == GROUPS - 1)
        def _():
            for c in normed_copies():
                c.wait()
            cot_copy().start()

    def cot_copy():
        return pltpu.make_async_copy(cot, normed.at[:, pl.ds(0, T)], cotsem.at[0])

    def live(s):
        pos = lax.broadcasted_iota(jnp.int32, (T, 1), 0) + at.z * T
        return jnp.where(pos < lengths[s], 1.0, 0.0)

    def normalise():
        for s in range(seqs):
            r = lax.rsqrt(ssq[s, :, 0:1] * (1.0 / DI) + EPS)
            for g in range(GROUPS):
                nyb[g, s * T : (s + 1) * T] = (ybuf[g, s] * r * gain[g, 6:7]).astype(bf16)
                ybuf[g, s] = jnp.zeros((T, CW), f32)
        pltpu.make_async_copy(nyb, ony, esem.at[seqs]).start()
        pltpu.make_async_copy(hin, ohin, esem.at[seqs + 1]).start()
        pltpu.make_async_copy(ssq, ossq, esem.at[seqs + 5]).start()
        cot_copy().wait()
        for s in range(seqs):
            normed[s, 0:T] = (live(s) * normed[s, 0:T].astype(f32)).astype(bf16)

    def out_chunk(c, carry):
        branch = dot(nyb[0], wo[c, :CW])
        for g in range(1, GROUPS):
            branch = branch + dot(nyb[g], wo[c, g * CW : (g + 1) * CW])
        branch = branch.reshape(seqs, T, CW)
        lane = pl.ds(pl.multiple_of(c * CW, 128), CW)
        masked = normed[:, 0:T, lane].reshape(rows, CW)
        for s in range(seqs):
            out[s, :, lane] = (tok[s, :, lane].astype(f32) + live(s) * branch[s]).astype(bf16)

        def upstream(g, carry):
            part = wo[c, pl.ds(pl.multiple_of(g * CW, 16), CW)]
            ybuf[g] += dot(masked, part, NT).reshape(seqs, T, CW)
            return carry

        lax.fori_loop(0, GROUPS, upstream, 0)

        @pl.when(c == NO - 1)
        def _():
            pltpu.make_async_copy(ybuf, odny, esem.at[0]).start()
            for s in range(seqs):
                t = jnp.zeros((T, 1), f32)
                for g in range(GROUPS):
                    t = t + jnp.sum(ybuf[g, s] * nyb[g, s * T : (s + 1) * T].astype(f32), axis=1, keepdims=True)
                tsum[s] = jnp.broadcast_to(t, (T, 128))
            pltpu.make_async_copy(tsum, otsum, esem.at[1]).start()

        return carry

    def keep(k, start):
        def f(src, dst):
            cp = pltpu.make_async_copy(src, dst, osem.at[k])
            cp.start() if start else cp.wait()

        @pl.when(in_i(k))
        def _():
            f(wi.at[chunk_i(k)], owin.at[chunk_i(k)])

    HOP = 3 if S <= 4 else 1
    last = at.m * LAG + 1

    def tick(t, carry):
        ga.send_z(t + AHEAD)
        for j in range(at.m + 1):
            ga.stage(t - j * LAG, j)
        k = t - last
        ga.arrived(k)
        keep(k, True)
        pl.when(k == 0)(unpack)
        pl.when(k == 1)(first_chunk)
        pl.when((k >= 2) & (k < MID))(lambda: values_chunk(k - 2, k - 1))
        g = k - 3 - HOP * at.z
        pl.when((g >= 0) & (g < GROUPS))(lambda: pass_state(g))
        pl.when((k >= GATE) & (k < LATE))(lambda: gate_chunk(k - GATE, k - GATE + 1 + GROUPS))

        pl.when(k == LATE)(normalise)
        late = jnp.clip(k - LATE, -1, NO - NO // 2 - 1)
        begin = jnp.where(late > 0, late + NO // 2, 0)
        end = jnp.where(late >= 0, late + NO // 2 + 1, 0)
        lax.fori_loop(begin, end, out_chunk, 0)

        return carry

    lax.fori_loop(0, n + last, tick, 0)

    def finish(k, carry):
        ga.sent(k)
        keep(k, False)
        return carry

    lax.fori_loop(0, n, finish, 0)

    @pl.when(at.z < S - 1)
    def _():
        halo_copy().wait_send()

        def f(g, carry):
            chain(g).wait_send()
            return carry

        lax.fori_loop(0, GROUPS, f, 0)

    for k in (GROUPS - 1, GROUPS):
        pltpu.make_async_copy(pcs.at[k % 2], opc.at[k], pcsem.at[k % 2]).wait()
    for g in (GROUPS - 2, GROUPS - 1):
        pltpu.make_async_copy(zst.at[g % 2], oz.at[g], zsem.at[g % 2]).wait()
    for c in prepared():
        c.wait()
    pltpu.make_async_copy(ybuf, odny, esem.at[0]).wait()
    pltpu.make_async_copy(tsum, otsum, esem.at[1]).wait()
    for i in (seqs * GROUPS - 2, seqs * GROUPS - 1):
        y_copy(i).wait()
    pltpu.make_async_copy(nyb, ony, esem.at[seqs]).wait()
    pltpu.make_async_copy(hin, ohin, esem.at[seqs + 1]).wait()
    pltpu.make_async_copy(convp, oconv, esem.at[seqs + 2]).wait()
    pltpu.make_async_copy(gain, ogain, esem.at[seqs + 3]).wait()
    pltpu.make_async_copy(ngain, ong, esem.at[seqs + 4]).wait()
    pltpu.make_async_copy(ssq, ossq, esem.at[seqs + 5]).wait()


def forward(S, dp, lengths, tok, win, wout, small, cot):
    PL = dp // 2
    nd = S * dp
    seqs, T, _ = tok.shape
    n = 1 + NI + NO
    rows = seqs * T
    sds = jax.ShapeDtypeStruct
    dma = pltpu.SemaphoreType.DMA
    V = pltpu.VMEM

    vm = pl.BlockSpec(memory_space=pltpu.VMEM)
    hb = pl.BlockSpec(memory_space=pl.ANY)
    wi_s, wo_s = (NI, D, CW), (NO, DI, CW)
    RI, RO = -(-(D // nd) // 16) * 16, -(-(DI // nd) // 16) * 16
    win = jnp.pad(win, ((0, RI - D // nd), (0, 0)))
    wout = jnp.pad(wout, ((0, RO - DI // nd), (0, 0)))
    zi_s = (NI, S, RI, CW) if RI * nd > D else (8, 128)
    zo_s = (NO, S, RO, CW) if RO * nd > DI else (8, 128)
    return pl.pallas_call(
        functools.partial(forward_kernel, S, PL),
        out_shape=[
            sds((seqs, T, D), bf16), sds(wi_s, bf16), sds((D // CW, rows, CW), bf16),
            sds((1 + GROUPS, seqs, HALO + T, CW), bf16), sds((seqs, T, 128), f32),
            sds((GROUPS, seqs, T, CW), f32), sds((GROUPS, seqs, T, CW), f32),
            sds((GROUPS, seqs, STATE, CW), bf16), sds((GROUPS, rows, CW), bf16),
            sds((1 + GROUPS, 8, CW), f32), sds((GROUPS, 8, CW), f32),
            sds((seqs, T, 128), f32), sds((8, D), f32), sds((GROUPS, seqs, T, CW), f32), sds((seqs, T, 128), f32),
            sds((2, seqs, T, 128), f32), sds((seqs, GROUPS, 8, T), f32), sds((seqs, T, T), f32),
            sds((seqs, T, 2 * STATE), bf16), sds((seqs, STATE, T), f32),
        ],
        in_specs=[pl.BlockSpec(memory_space=pltpu.SMEM)] + [vm] * 9 + [hb] * 2,
        out_specs=[vm] + [hb] * 19,
        scratch_shapes=[
            V(wi_s, bf16), V(wo_s, bf16), V((nd * 16, 128), bf16), V(zi_s, bf16), V(zo_s, bf16), V((seqs, HALO, D), bf16),
            V((seqs, HALO + T, D), bf16), V((GROUPS, seqs, T, CW), f32), V((GROUPS, rows, CW), bf16),
            V((GROUPS, seqs, STATE, CW), f32), V((GROUPS, seqs, STATE, CW), bf16),
            V((GROUPS, seqs, STATE, CW), bf16), V((GROUPS, seqs, 8, CW), f32), V((seqs, T, T), f32),
            V((seqs, STATE, T), f32), V((seqs, T, 2 * STATE), bf16), V((seqs, T, 2 * STATE), bf16),
            V((seqs, STATE, T), f32), V((2, seqs, T, 128), f32),
            V((seqs, GROUPS, 8, T), f32), V((1 + GROUPS, 8, CW), f32), V((GROUPS, 8, CW), f32), V((8, D), f32),
            V((seqs, T, 128), f32), V((seqs, T, 128), f32), V((8, 128), f32), V((2, seqs, HALO + T, CW), bf16),
            V((2, seqs, T, CW), f32), V((2, T, CW), f32),
            dma((NO,)), dma((n,)), dma((2,)), dma((2, GROUPS)), dma((2,)), dma((2,)), dma((2,)), dma((seqs + 11,)), dma((D // CW, seqs)), dma((1,)),
            dma((n, S - 1)), dma((n, S - 1)), dma((n, 2 * PL - 2)), dma((n, 2 * PL - 2)), dma((n, 2 * PL)), dma((n, 2 * PL)),
        ],
        name="forward",
        compiler_params=pltpu.CompilerParams(collective_id=0, has_side_effects=True, vmem_limit_bytes=63 << 20),
    )(lengths, tok, win, *small, wout, cot)


class Scatter:
    def __init__(self, at, R, bufs, sems):
        self.at, self.R, self.SR = at, R, at.S * R
        self.acc, self.cS, self.cR, self.xS, self.xR, self.zS, self.zR, self.zown = bufs
        self.cs, self.cr, self.xs, self.xr, self.zs, self.zr = sems
        self.NA, self.NS, self.NB = self.acc.shape[0], self.xS.shape[0], self.xR.shape[0]
        self.NC, self.MC = self.cR.shape[0], self.cS.shape[0]
        self.NZ, self.MZ = self.zR.shape[0], self.zS.shape[0]
        self.kind = self.xS.dtype

    def ccopy(self, k):
        at, i, o = self.at, lax.rem(k, self.MC), lax.rem(k, self.NC)
        return remote(self.cS.at[i], self.cR.at[o], self.cs.at[i], self.cr.at[o], (at.sib, at.z))

    def xcopy(self, k, j, i, h):
        at, n = self.at, 2**j - 1 + i
        a, b = lax.rem(k, self.NS), lax.rem(k, self.NB)
        return remote(self.xS.at[a, h, n], self.xR.at[b, h, n], self.xs.at[a, h, n], self.xr.at[b, h, n], at.across(j, h))

    def zcopy(self, k, o):
        at = self.at
        a, b = lax.rem(k, self.MZ), lax.rem(k, self.NZ)
        return remote(self.zS.at[a, lax.rem(at.z + o, at.S)], self.zR.at[b, o - 1], self.zs.at[a, o - 1],
                      self.zr.at[b, o - 1], at.along(o))

    def ready(self, k, slots, wait):
        if isinstance(k, int):
            if k >= slots:
                wait()
        else:
            pl.when(k >= slots)(wait)

    def produce(self, k, sibling, own):
        self.ready(k, self.MC, lambda: self.ccopy(k - self.MC).wait_send())
        a, n = lax.rem(k, self.MC), lax.rem(k, self.NA)
        sibling(self.cS.at[a])
        self.ccopy(k).start()
        own(self.acc.at[n])

    def send_x(self, k, j):
        at, n, a, half = self.at, lax.rem(k, self.NA), lax.rem(k, self.NS), self.SR // 2
        for h in range(2):
            for i in range(2**j):
                self.ready(k, self.NS, lambda: self.xcopy(k - self.NS, j, i, h).wait_send())
                q = flip(at.held(h, j)[i], at.weight(j, h))
                self.xS[a, h, 2**j - 1 + i] = self.acc[n, q, h * half : (h + 1) * half].astype(self.kind)
                self.xcopy(k, j, i, h).start()

    def stage_c(self, k):
        self.ccopy(k).wait_recv()
        n, o = lax.rem(k, self.NA), lax.rem(k, self.NC)
        for q in range(self.at.PL):
            self.acc[n, q] += self.cR[o, q]
        self.send_x(k, self.at.m - 1)

    def stage_x(self, k, j):
        at, n, b, half = self.at, lax.rem(k, self.NA), lax.rem(k, self.NB), self.SR // 2
        for h in range(2):
            for i in range(2**j):
                self.xcopy(k, j, i, h).wait_recv()
                q = at.held(h, j)[i]
                self.acc[n, q, h * half : (h + 1) * half] += self.xR[b, h, 2**j - 1 + i].astype(f32)
        if j > 0:
            self.send_x(k, j - 1)
            return
        a = lax.rem(k, self.MZ)
        for o in range(1, at.S):
            self.ready(k, self.MZ, lambda: self.zcopy(k - self.MZ, o).wait_send())
        v = self.acc[n, at.p]
        padded = self.zS.shape[2]
        if padded == self.R:
            self.zS[a] = v.astype(self.kind).reshape(at.S, self.R, v.shape[1])
        else:
            spread_rows = dot(picks(self.SR, self.R, padded), v.astype(bf16), ((0,), (0,)))
            self.zS[a] = spread_rows.astype(self.kind).reshape(at.S, padded, v.shape[1])
        for o in range(1, at.S):
            self.zcopy(k, o).start()
        if padded == self.R:
            own = self.acc[n, at.p, pl.ds(pl.multiple_of(at.z * self.R, 8), self.R)]
        else:
            i = lax.broadcasted_iota(jnp.int32, (padded, self.SR), 0)
            j = lax.broadcasted_iota(jnp.int32, (padded, self.SR), 1)
            mine = (i < self.R) & (j == i + at.z * self.R)
            own = dot(jnp.where(mine, 1.0, 0.0), v, precision=HIGH)
        self.zown[a] = own

    def stage_z(self, k):
        b = lax.rem(k, self.NZ)
        total = self.zown[lax.rem(k, self.MZ)]
        for o in range(1, self.at.S):
            self.zcopy(k, o).wait_recv()
            total = total + self.zR[b, o - 1].astype(f32)
        return total

    def drain(self, n):
        for k in range(max(0, n - self.MC), n):
            self.ccopy(k).wait_send()
        for k in range(max(0, n - self.NS), n):
            for h in range(2):
                for j in range(self.at.m):
                    for i in range(2**j):
                        self.xcopy(k, j, i, h).wait_send()
        for k in range(max(0, n - self.MZ), n):
            for o in range(1, self.at.S):
                self.zcopy(k, o).wait_send()


def scatter_scratch(S, PL, R, padded, width, kind, many, lag, zlag):
    m = PL.bit_length() - 1
    SR = S * R
    NS, NB, NC, NA, MZ, NZ = (lag + 1, 2 * lag, 2, 1 + m * lag, zlag + 1, 2 * zlag) if many else (1,) * 6
    V, dma = pltpu.VMEM, pltpu.SemaphoreType.DMA
    bufs = [
        V((NA, PL, SR, width), f32), V((1, PL, SR, width), f32), V((NC, PL, SR, width), f32),
        V((NS, 2, PL - 1, SR // 2, width), kind), V((NB, 2, PL - 1, SR // 2, width), kind),
        V((MZ, S, padded, width), kind), V((NZ, S - 1, padded, width), kind), V((MZ, padded, width), f32),
    ]
    sems = [dma((1,)), dma((NC,)), dma((NS, 2, PL - 1)), dma((NB, 2, PL - 1)), dma((MZ, S - 1)), dma((NZ, S - 1))]
    return bufs, sems


def pair(cols, q):
    T = cols.shape[0]
    low = lax.broadcasted_iota(jnp.int32, (T, 128), 1) < HDIM
    first = jnp.broadcast_to(cols[:, 2 * q : 2 * q + 1], (T, 128))
    second = jnp.broadcast_to(cols[:, 2 * q + 1 : 2 * q + 2], (T, 128))
    return jnp.where(low, first, second)


def pair_sums(v, q):
    hi = v.astype(bf16)
    rest = v - hi.astype(f32)
    mid = rest.astype(bf16)
    low = (rest - mid.astype(f32)).astype(bf16)
    ch = lax.broadcasted_iota(jnp.int32, (128, 128), 0)
    hd = lax.broadcasted_iota(jnp.int32, (128, 128), 1) - 2 * q
    ones = jnp.where((ch >= hd * HDIM) & (ch < hd * HDIM + HDIM), 1.0, 0.0).astype(bf16)
    return dot(jnp.concatenate([hi, mid, low], axis=1), jnp.concatenate([ones, ones, ones], axis=0))


def turned_back(x, g):
    return pltpu.roll(x, GH * g, 1)


def backward_kernel(S, PL, RLAG, ZLAG, lengths, decay, bias, skips, ngain, gain, convp, raw, ssq, tsum, ld, ldT, gram, keys2, readsT,
                    tok, cot, hin, norm_in, ny, win, zin, yin, dyin, pcin,
                    tgrad, ghead, gin, gout, gsm,
                    masked, lhsT, dyb, dzb, loc, dsin, dsout, dn, dgram, dkeys, dreads,
                    dld, dst, cvec, gvec, hvec, nxt, dcv, fin, heads, pc0, wib, zb, yb, db, hb, pcb,
                    wisem, zsem, ysem, dsem, hinsem, pcsem, setsem, finsem, chsem, hasem, *rest):
    at = Place(S, PL)
    seqs, T, _ = raw.shape
    rows = seqs * T
    nd = S * PL * 2
    R = D // nd
    SR = S * R
    H = T // 2
    NQ = 2 * GROUPS + 1 + 2 * NO
    big = Scatter(at, R, rest[:8], rest[8:14])
    tiny = Scatter(at, 16, rest[14:22], rest[22:28])
    sg = rest[28]
    HOP = 2 if S <= 4 else 1
    TB = 2 + HOP * (S - 1)

    def wi_copy(i):
        a = lax.rem(i, 2)
        k = 9 + i - 16 * lax.div(i, 8) + 7 * lax.div(i, 16)
        return pltpu.make_async_copy(win.at[k], wib.at[a], wisem.at[a])

    def item(i):
        return lax.rem(lax.div(i, seqs), GROUPS), lax.rem(i, seqs)

    def y_copy(i):
        a = lax.rem(i, 2)
        return pltpu.make_async_copy(yin.at[item(i)], yb.at[a], ysem.at[a])

    def zy_copies(i):
        a = lax.rem(i, 2)
        return (pltpu.make_async_copy(zin.at[item(i)], zb.at[a], zsem.at[a]),
                pltpu.make_async_copy(dyin.at[item(i)], db.at[a], dsem.at[a]), y_copy(i))

    def b_copies(g):
        a = lax.rem(g, 2)
        return (pltpu.make_async_copy(hin.at[g], hb.at[a], hinsem.at[a]),
                pltpu.make_async_copy(pcin.at[g + 1], pcb.at[a], pcsem.at[a]))

    def begin(copies, when=True):
        if when is True:
            for c in copies:
                c.start()
        else:
            @pl.when(when)
            def _():
                for c in copies:
                    c.start()

    NCH = D // CW
    setup = [pltpu.make_async_copy(cot, tgrad, setsem.at[0]), pltpu.make_async_copy(ny, dzb, setsem.at[1])]
    setup.append(pltpu.make_async_copy(pcin.at[0], pc0, setsem.at[2 + NCH]))
    setup += [pltpu.make_async_copy(norm_in.at[c], wib.at[c // 3, pl.ds(c % 3 * rows, rows)], setsem.at[2 + c])
              for c in range(NCH)]
    begin([*setup, *zy_copies(0), *b_copies(0)])
    set_heads(heads, decay, bias, skips)
    at.barrier()
    for c in setup:
        c.wait()

    for s in range(seqs):
        live = jnp.where(lax.broadcasted_iota(jnp.int32, (T, 1), 0) + at.z * T < lengths[s], 1.0, 0.0)
        masked[s * T : (s + 1) * T] = (live * tgrad[s].astype(f32)).astype(bf16)
    perm = lax.broadcasted_iota(jnp.int32, (2 * SR, 2 * SR), 0)
    perm_j = lax.broadcasted_iota(jnp.int32, (2 * SR, 2 * SR), 1)
    take = jnp.zeros(perm.shape, jnp.bool_)
    for h in range(2):
        for b in range(S):
            inside = (perm >= h * SR + b * R) & (perm < h * SR + b * R + R)
            take = take | (inside & (perm_j - (2 * b + h) * R == perm - (h * SR + b * R)))
    take = jnp.where(take, 1.0, 0.0).astype(bf16)
    same = jnp.where(lax.broadcasted_iota(jnp.int32, (SR, SR), 0) == lax.broadcasted_iota(jnp.int32, (SR, SR), 1),
                     1.0, 0.0).astype(bf16)
    for q in range(PL):
        for cls in range(2):
            cc = 1 - at.c if cls == 0 else at.c
            slab = 2 * q + cls
            for s in range(seqs):
                tl = slice(s * T, (s + 1) * T)
                lane = slab * 2 * SR
                r = dot(take, dzb[lane // CW, tl, lane % CW : lane % CW + 2 * SR], NT).astype(bf16)
                lhsT[0, cc, q * SR : (q + 1) * SR, tl] = r[:SR]
                lhsT[1, cc, q * SR : (q + 1) * SR, tl] = r[SR:]

    def turn_normed():
        for q in range(PL):
            for cls in range(2):
                cc = 1 - at.c if cls == 0 else at.c
                lane, c = (2 * q + cls) * SR % CW, (2 * q + cls) * SR // CW
                for s in range(seqs):
                    part = wib[c // 3, c % 3 * rows + s * T : c % 3 * rows + (s + 1) * T, lane : lane + SR]
                    lhsT[2, cc, q * SR : (q + 1) * SR, s * T : (s + 1) * T] = dot(same, part, NT).astype(bf16)
        begin([wi_copy(0)])


    for ref in (dn, dgram, dkeys, dreads, dld, dst, cvec, gvec, hvec, sg):
        ref[...] = jnp.zeros_like(ref)

    @pl.when(at.z == S - 1)
    def _():
        dsin[...] = jnp.zeros_like(dsin)
        nxt[...] = jnp.zeros_like(nxt)

    def rms(s):
        return lax.rsqrt(ssq[s, :, 0:1] * (1.0 / DI) + EPS)

    def through_gate(g, carry):
        def sequence(s, carry):
            i = g * seqs + s
            a = lax.rem(i, 2)
            for c in zy_copies(i):
                c.wait()
            begin(zy_copies(i + 1)[:2], i + 1 < seqs * GROUPS)
            begin([y_copy(i + 1)])
            r = rms(s)
            z, y, dn_y = zb[a], yb[a], db[a]
            sg_ = sigmoid(z)
            gate = z * sg_
            w = (y * gate) * r
            gvec[g, 6:7] += jnp.sum(dn_y * w, axis=0, keepdims=True)
            dw = r * (dn_y * gain[g, 6:7] - w * (tsum[s, :, 0:1] * (1.0 / DI)))
            dzb[g, pl.ds(pl.multiple_of(s * T, 16), T)] = (dw * y * (sg_ * (1.0 + z * (1.0 - sg_)))).astype(bf16)
            dy = dw * gate
            dyb[g, s] = dy
            loc[g, s] = dot(readsT[s], dy * jnp.exp(spread(turned(ld[0, s], g), g)), precision=HIGH)
            return carry

        lax.fori_loop(0, seqs, sequence, 0)
        return 0

    def chain(g):
        return remote(dsout.at[g], dsin.at[g], chsem.at[0, g], chsem.at[1, g], at.along(S - 1))

    def pass_state(g):
        @pl.when(at.z < S - 1)
        def _():
            chain(g).wait_recv()

        @pl.when(at.z > 0)
        def _():
            for s in range(seqs):
                last = jnp.exp(spread(turned(ld[0, s, T - 8 :], g), g))[7:8]
                dsout[g, s] = (last * dsin[g, s].astype(f32) + loc[g, s]).astype(bf16)
            chain(g).start()

    def edge(g):
        return remote(dyb.at[g, :, pl.ds(0, 8)], nxt.at[g], hasem.at[0, g], hasem.at[1, g], at.along(S - 1))

    def conv_sums(g, x, dm, lanes):
        x = x[:, :lanes]
        for k in range(CONV):
            shifted = x[HALO:] if k == CONV - 1 else pltpu.roll(x, CONV - 1 - k, 0)[HALO:]
            cvec[g, k : k + 1, :lanes] += jnp.sum(dm * shifted, axis=0, keepdims=True)
        cvec[g, CONV : CONV + 1, :lanes] += jnp.sum(dm, axis=0, keepdims=True)

    def recurrence(i, carry):
        g, s = lax.div(i, seqs), lax.rem(i, seqs)
        a = lax.rem(g, 2)

        @pl.when(s == 0)
        def _():
            for c in b_copies(g):
                c.wait()
            begin(b_copies(g + 1), g + 1 < GROUPS)

        y_copy(i).wait()
        begin([y_copy(i + 1)], i + 1 < seqs * GROUPS)

        cp = convp[g + 1]
        low = lax.broadcasted_iota(jnp.int32, (T, 128), 1) < HDIM
        is_last = lax.broadcasted_iota(jnp.int32, (T, 128), 0) == T - 1
        skips = turned(jnp.broadcast_to(heads[2:3], (8, 128)), g)
        ldc, ldr, stc = turned(ld[0, s], g), ldT[s, g], turned(ld[1, s], g)
        dgt, dgb = jnp.zeros((H, H), f32), jnp.zeros((H, T), f32)
        sums, dk, dr = jnp.zeros((2 * T, 128), f32), jnp.zeros((T, STATE), f32), jnp.zeros((T, STATE), f32)
        for q in range(GH // 2):
            sl = slice(q * 128, q * 128 + 128)
            skip = pair(skips, q)[0:1]
            x = pcb[a, s, :, sl].astype(f32)
            mixed = convolve(x, cp[:, sl])
            sg_ = sigmoid(mixed)
            V = mixed * sg_
            lde, st = pair(ldc, q), pair(stc, q)
            last = lde[T - 1 : T]
            tail = jnp.exp(last - lde)
            X = V * st
            dS, hq = dsin[g, s, :, sl], hb[a, s, :, sl]
            dXt = tail * dot(keys2[s], jnp.concatenate([dS, dS], axis=0))
            dY = dyb[g, s, :, sl]
            xh = X.astype(bf16)
            x2 = jnp.concatenate([xh, xh], axis=1)
            dyp = jnp.concatenate(halves(dY), axis=1)
            two = []
            for h in (2 * q, 2 * q + 1):
                ft = fade(ldc, ldr, h, 0, H, H)
                fb = fade(ldc, ldr, h, H, H, T)
                mt = (gram[s, :H, :H] * ft).astype(bf16)
                mb = (gram[s, H:, :] * fb).astype(bf16)
                r0 = dot(jnp.concatenate([mt, mb[:, :H]], axis=0), dyp, TN)
                r1 = dot(mb[:, H:], dyp[H:], TN)
                r = jnp.concatenate([r0, r1], axis=0)
                two.append(r[:, :128] + r[:, 128:])
                mine = low if h == 2 * q else jnp.logical_not(low)
                dyh = jnp.concatenate(halves(jnp.where(mine, dY, 0.0)), axis=1)
                dgt = dgt + ft * dot(dyh[:H], x2[:H], NT)
                dgb = dgb + fb * dot(dyh[H:], x2, NT)
            dX = jnp.where(low, two[0], two[1]) + dXt
            dV = st * dX + skip * dY
            gvec[g, 7:8, sl] += jnp.sum(dY * V, axis=0, keepdims=True)
            q1 = dY * (yb[lax.rem(i, 2), :, sl] - skip * V) - X * dX
            at_end = jnp.sum(X * dXt, axis=0, keepdims=True) + jnp.exp(last) * jnp.sum(
                hq.astype(f32) * dS.astype(f32), axis=0, keepdims=True)
            q1 = q1 + jnp.where(is_last, at_end, 0.0)
            sums = sums + pair_sums(jnp.concatenate([q1, dX * V], axis=0), q)
            dk = dk + dot(jnp.concatenate(halves(tail * X), axis=1), jnp.concatenate([dS, dS], axis=1), NT)
            dr = dr + dot(jnp.concatenate(halves(dY * jnp.exp(lde)), axis=1), jnp.concatenate([hq, hq], axis=1), NT)
            dm = dV * (sg_ * (1.0 + mixed * (1.0 - sg_)))
            dyb[g, s, :, sl] = dm
            for k in range(CONV):
                shifted = x[HALO:] if k == CONV - 1 else pltpu.roll(x, CONV - 1 - k, 0)[HALO:]
                cvec[g + 1, k : k + 1, sl] += jnp.sum(dm * shifted, axis=0, keepdims=True)
            cvec[g + 1, CONV : CONV + 1, sl] += jnp.sum(dm, axis=0, keepdims=True)
        dgram[s, :H, :H] += dgt
        dgram[s, H:, :] += dgb
        dld[s] += turned_back(sums[:T], g)
        dst[s] += turned_back(sums[T:], g)
        dkeys[s] += dk
        dreads[s] += dr

        @pl.when((at.z > 0) & (s == seqs - 1))
        def _():
            edge(g).start()

        return carry

    def unconvolve(dm, after, cp):
        ext = jnp.concatenate([dm, after], axis=0)
        n = ext.shape[0]
        out = cp[3:4] * dm
        for k in range(CONV - 1):
            out = out + cp[k : k + 1] * pltpu.roll(ext, n - (CONV - 1 - k), 0)[: dm.shape[0]]
        return out

    def heads_chunk():
        tri = lax.broadcasted_iota(jnp.int32, (T, T), 1) >= lax.broadcasted_iota(jnp.int32, (T, T), 0)
        tri = jnp.where(tri, 1.0, 0.0)
        cp = convp[0]
        for s in range(seqs):
            x = pc0[s].astype(f32)
            mixed = convolve(x, cp)[:, : 2 * STATE]
            sg_ = sigmoid(mixed)
            act = mixed * sg_
            keys, reads = act[:, :STATE], act[:, STATE:]
            dr = dreads[s] + dot(dgram[s], keys, precision=HIGH)
            dk = dkeys[s] + dot(dgram[s], reads, TN, HIGH)
            dm = jnp.concatenate([dk, dr], axis=1) * (sg_ * (1.0 + mixed * (1.0 - sg_)))
            conv_sums(0, x, dm, 2 * STATE)
            da = dot(tri, dld[s], precision=HIGH)
            draw = (dst[s] + da * heads[1:2]) * sigmoid(raw[s] + heads[0:1])
            hvec[0:1] += jnp.sum(da * ld[1, s], axis=0, keepdims=True) * heads[1:2]
            hvec[1:2] += jnp.sum(draw, axis=0, keepdims=True)
            zb[s] = jnp.concatenate([dm, draw], axis=1)

        @pl.when(at.z > 0)
        def _():
            kr_edge().start()

    def kr_edge():
        return remote(zb.at[:, pl.ds(0, 8)], nxt.at[GROUPS], hasem.at[0, GROUPS], hasem.at[1, GROUPS], at.along(S - 1))

    def terms(k):
        rhs = dcv[...]
        lhs = lhsT.at[jnp.minimum(lax.div(k, NO), 2)]

        def product(cc, ref):
            for lo in range(0, PL * SR, 384):
                ref[lo // SR : (lo + 384) // SR] = dot(lhs[cc, lo : lo + 384], rhs).reshape(384 // SR, SR, CW)

        def sibling(ref):
            product(0, ref)

        def own(ref):
            product(1, ref)

        big.produce(k, sibling, own)

    def back_in(i, d):
        wi_copy(i).wait()
        begin([wi_copy(i + 1)], i + 1 < 2 * GROUPS + 1)
        for lane in range(0, D, 512):
            dn[:, lane : lane + 512] += dot(d, wib[lax.rem(i, 2), lane : lane + 512], NT)

    def out_terms(k):
        c = lax.rem(k, NO)
        dcv[...] = masked[:, pl.ds(pl.multiple_of(c * CW, 128), CW)]

    def gate_terms(k):
        dcv[...] = dzb[k - 2 * NO]

    def value_terms(k):
        g = k - 2 * NO - GROUPS

        @pl.when(at.z < S - 1)
        def _():
            edge(g).wait_recv()

        cp = convp[g + 1]
        for s in range(seqs):
            dcv[s * T : (s + 1) * T] = unconvolve(dyb[g, s], nxt[g, s], cp).astype(bf16)

    def first_terms(k):
        @pl.when(at.z < S - 1)
        def _():
            kr_edge().wait_recv()

        cp = convp[0]
        for s in range(seqs):
            v = zb[s]
            c = unconvolve(v, nxt[GROUPS, s], cp)
            is_conv = lax.broadcasted_iota(jnp.int32, (T, CW), 1) < 2 * STATE
            dcv[s * T : (s + 1) * T] = jnp.where(is_conv, c, v).astype(bf16)

    def place(vec, count, first):
        lo, hi = first // count, min(nd - 1, (first + CW - 1) // count)
        who = (lax.broadcasted_iota(jnp.int32, (hi - lo + 1, 1, CW), 0) + lo) * count
        ch = lax.broadcasted_iota(jnp.int32, (hi - lo + 1, 1, CW), 2) + first
        wide = jnp.where((ch >= who) & (ch < who + count), vec[None], 0.0).reshape(-1, CW)
        cols = columns(count, first)
        sg[lo : hi + 1, 0:8] += dot(wide, cols, NT, HIGH).reshape(hi - lo + 1, 8, 128)

    def place_group(g):
        row = lax.broadcasted_iota(jnp.int32, (8, CW), 0)
        place(cvec[1 + g], CONV_CH // nd, g * CW)
        place(jnp.where(row == 6, gvec[g], 0.0), DI // nd, g * CW)
        per_head = pair_sums(gvec[g, :, :128], 0)
        for q in range(1, GH // 2):
            per_head = per_head + pair_sums(gvec[g, :, q * 128 : q * 128 + 128], q)
        hvec[2:3] += turned_back(per_head, g)[7:8]

    def ending():
        tok_copy().wait()
        ng = jnp.zeros((1, D), f32)
        for s in range(seqs):
            for i in range(0, T, 64):
                u = masked[s * T + i : s * T + i + 64].astype(f32)
                r = lax.rsqrt(jnp.sum(u * u, axis=1, keepdims=True) * (1.0 / D) + EPS)
                dnv = dn[s * T + i : s * T + i + 64]
                ng = ng + jnp.sum(dnv * u * r, axis=0, keepdims=True)
                v = dnv * ngain[0:1]
                mean = jnp.sum(v * u, axis=1, keepdims=True) * (1.0 / D)
                tgrad[s, i : i + 64] = (tgrad[s, i : i + 64].astype(f32) + r * v - u * (r * r * r * mean)).astype(bf16)
        row = lax.broadcasted_iota(jnp.int32, (8, CW), 0)
        place(cvec[0], CONV_CH // nd, DI)
        for g in range(D // CW):
            place(jnp.where(row == 5, ng[:, g * CW : (g + 1) * CW], 0.0), D // nd, g * CW)
        sg[:, 8:16] = jnp.broadcast_to(hvec[...][None], (nd, 8, 128))

        def sibling(ref):
            for q in range(PL):
                ref[q] = sg[pl.ds((2 * q + 1 - at.c) * S, S)].reshape(S * 16, 128)

        def own(ref):
            for q in range(PL):
                ref[q] = sg[pl.ds((2 * q + at.c) * S, S)].reshape(S * 16, 128)

        tiny.produce(0, sibling, own)

    def tok_copy():
        return pltpu.make_async_copy(tok, masked, setsem.at[0])

    def fin_copy(k, gate):
        a = lax.rem(k, 2)
        if gate:
            return pltpu.make_async_copy(fin.at[a], gin.at[:, pl.ds(pl.multiple_of((k - 2 * NO) * CW, 128), CW)], finsem.at[a])
        return pltpu.make_async_copy(
            fin.at[a], gout.at[lax.div(k, NO), :, pl.ds(pl.multiple_of(lax.rem(k, NO) * CW, 128), CW)], finsem.at[a])

    def each_fin(k, f):
        pl.when(k < 2 * NO)(lambda: f(fin_copy(k, False)))
        pl.when(k >= 2 * NO)(lambda: f(fin_copy(k, True)))

    def finish(k):
        @pl.when(k >= 2)
        def _():
            each_fin(k - 2, lambda c: c.wait())

        fin[lax.rem(k, 2)] = big.stage_z(k)
        each_fin(k, lambda c: c.start())

    m = at.m

    def inside(k):
        return (k >= 0) & (k < NQ)

    def tick(t, carry):
        pl.when(inside(t - 1 - m * RLAG - ZLAG))(lambda: finish(t - 1 - m * RLAG - ZLAG))
        for j in range(m):
            k = t - 1 - (m - j) * RLAG
            pl.when(inside(k))(lambda: big.stage_x(k, j))
        pl.when(inside(t - 1))(lambda: big.stage_c(t - 1))
        pl.when(t < 2 * NO)(lambda: out_terms(t))
        pl.when((t >= 2 * NO) & (t < 2 * NO + GROUPS))(lambda: gate_terms(t))
        pl.when((t >= 2 * NO + GROUPS) & (t < NQ - 1))(lambda: value_terms(t))
        pl.when(t == NQ - 1)(lambda: first_terms(t))
        pl.when(t < NQ)(lambda: terms(t))
        pl.when((t >= 2 * NO + GROUPS) & (t < NQ))(lambda: back_in(t - 2 * NO, dcv[...]))

        pl.when(t == 1)(turn_normed)

        @pl.when(t < GROUPS // 2)
        def _():
            lax.fori_loop(2 * t, 2 * t + 2, through_gate, 0)

        @pl.when((t >= GROUPS // 2) & (t < GROUPS))
        def _():
            def both(g, carry):
                back_in(g, dzb[g])
                return carry

            lax.fori_loop(2 * t - GROUPS, 2 * t - GROUPS + 2, both, 0)

        step = t - 1 - HOP * (S - 1 - at.z)
        passed = lax.div(2 * step + 2, 3)
        pl.when((step >= 0) & (lax.rem(step, 3) < 2) & (passed < GROUPS))(lambda: pass_state(passed))
        def parts_before(t):
            return lax.div(jnp.clip(t - TB, 0, NQ - 2 - TB) * seqs * GROUPS + NQ - 3 - TB, NQ - 2 - TB)

        lax.fori_loop(parts_before(t), parts_before(t + 1), recurrence, 0)
        pl.when(t == 2 * NO)(lambda: tok_copy().start())
        pl.when(t == NQ - 2)(heads_chunk)
        for g in range(GROUPS):
            pl.when(t == 2 * NO + GROUPS + g)(lambda: place_group(g))
        pl.when(t == NQ)(ending)
        pl.when(t == NQ + 1)(lambda: tiny.stage_c(0))
        for j in range(m):
            pl.when(t == NQ + 1 + m - j)(lambda: tiny.stage_x(0, j))
        return carry

    lax.fori_loop(0, NQ + 1 + max(1 + m, m * RLAG + ZLAG), tick, 0)
    total = tiny.stage_z(0)
    gsm[...] = total[:8]
    ghead[...] = total[8:]
    tiny.drain(1)
    big.drain(NQ)
    for k in (NQ - 2, NQ - 1):
        fin_copy(k, True).wait()

    def sent(g, carry):
        chain(g).wait_send()
        edge(g).wait_send()
        return carry

    @pl.when(at.z > 0)
    def _():
        lax.fori_loop(0, GROUPS, sent, 0)
        kr_edge().wait_send()


def backward(S, dp, lengths, tok, cot, small, saved):
    (owin, onormed, opc, oraw, oz, oy, ohin, ony, oconv, ogain, ossq, ong, odny, otsum, old, oldT, ogram, okeys2,
     oreadsT) = saved
    PL = dp // 2
    RLAG, ZLAG = (2, 3) if PL <= 4 else (1, 1)
    nd = S * dp
    R = D // nd
    Rp = -(-R // 16) * 16
    SR = S * R
    seqs, T, _ = tok.shape
    rows = seqs * T
    sds = jax.ShapeDtypeStruct
    dma = pltpu.SemaphoreType.DMA
    V = pltpu.VMEM
    vm = pl.BlockSpec(memory_space=pltpu.VMEM)
    hb = pl.BlockSpec(memory_space=pl.ANY)
    bufs, sems = scatter_scratch(S, PL, R, Rp, CW, bf16, True, RLAG, ZLAG)
    tbufs, tsems = scatter_scratch(S, PL, 16, 16, 128, f32, False, 1, 1)
    return pl.pallas_call(
        functools.partial(backward_kernel, S, PL, RLAG, ZLAG),
        out_shape=[sds((seqs, T, D), bf16), sds((8, 128), f32), sds((Rp, NI * CW), f32), sds((2, Rp, D), f32), sds((8, 128), f32)],
        in_specs=[pl.BlockSpec(memory_space=pltpu.SMEM)] + [vm] * 14 + [hb] * 10,
        out_specs=[vm, vm, hb, hb, vm],
        scratch_shapes=[
            V((rows, D), bf16), V((3, 2, PL * SR, rows), bf16),
            V((GROUPS, seqs, T, CW), f32), V((GROUPS, rows, CW), bf16), V((GROUPS, seqs, STATE, CW), f32),
            V((GROUPS, seqs, STATE, CW), bf16), V((GROUPS, seqs, STATE, CW), bf16), V((rows, D), f32),
            V((seqs, T, T), f32), V((seqs, T, STATE), f32), V((seqs, T, STATE), f32),
            V((seqs, T, 128), f32), V((seqs, T, 128), f32),
            V((1 + GROUPS, 8, CW), f32), V((GROUPS, 8, CW), f32), V((8, 128), f32),
            V((1 + GROUPS, seqs, 8, CW), f32), V((rows, CW), bf16),
            V((2, Rp, CW), f32), V((8, 128), f32), V((seqs, HALO + T, CW), bf16),
            V((2, D, CW), bf16), V((2, T, CW), f32), V((2, T, CW), f32), V((2, T, CW), f32),
            V((2, seqs, STATE, CW), bf16), V((2, seqs, HALO + T, CW), bf16),
            dma((2,)), dma((2,)), dma((2,)), dma((2,)), dma((2,)), dma((2,)), dma((3 + D // CW,)), dma((2,)), dma((2, GROUPS)), dma((2, GROUPS + 1)),
            *bufs, *sems, *tbufs, *tsems, V((nd, 16, 128), f32),
        ],
        name="backward",
        compiler_params=pltpu.CompilerParams(collective_id=1, has_side_effects=True, vmem_limit_bytes=127 << 19),
    )(lengths, *small[4:], ong, ogain, oconv, oraw, ossq, otsum, old, oldT, ogram, okeys2, oreadsT,
      tok.reshape(rows, D), cot, ohin, onormed, ony, owin, oz, oy, odny, opc)


def deliver_kernel(out, tgrad, gout, gin, gsm, ghead, *results):
    for src, dst in zip((out, tgrad, gout), results):
        dst[...] = src[...]
    results[3][...] = gin[:, :PROJ]
    cw, cb, ng, gg, decay, bias, skip = results[4:]
    cw[...] = gsm[0:CONV, : cw.shape[1]]
    for ref, r in ((cb, 4), (ng, 5), (gg, 6)):
        ref[...] = gsm[r : r + 1, : ref.shape[1]]
    for ref, r in ((decay, 0), (bias, 1), (skip, 2)):
        ref[...] = ghead[r : r + 1, : ref.shape[1]]


def deliver(nd, *arrays):
    sds = jax.ShapeDtypeStruct
    vm = pl.BlockSpec(memory_space=pltpu.VMEM)
    widths = (CONV_CH // nd, D // nd, DI // nd, HEADS, HEADS, HEADS)
    return pl.pallas_call(
        deliver_kernel,
        out_shape=[sds(a.shape, a.dtype) for a in arrays[:3]] + [sds((arrays[3].shape[0], PROJ), f32)] + [sds((CONV, CONV_CH // nd), f32)] + [sds((1, w), f32) for w in widths],
        in_specs=[vm] * 6,
        out_specs=[vm] * 11,
        name="deliver",
        compiler_params=pltpu.CompilerParams(vmem_limit_bytes=32 << 20),
    )(*arrays)


def body(tokens, lengths, in_weight, conv_weight, conv_bias, decay_log, step_bias, skip_gain, norm_gain, gate_gain,
         out_weight, cotangent):
    S, dp = lax.axis_size("seq"), lax.axis_size("dp")
    nd = S * dp
    row = lambda v: v.reshape(1, -1)
    small = [conv_weight.T, *map(row, (conv_bias, norm_gain, gate_gain, decay_log, step_bias, skip_gain))]
    out, *saved = forward(S, dp, lengths, tokens, in_weight, out_weight, small, cotangent)
    tgrad, ghead, gin, gout, gsm = backward(S, dp, lengths, tokens, cotangent, small, saved)
    R = D // nd
    if gin.shape[0] > R:
        gin, gout = gin[:R], gout[:, :R]
    out, tgrad, gout, gin, cw, *rows = deliver(nd, out, tgrad, gout, gin, gsm, ghead)
    cb, ng, gg, decay, bias, skip = (r.reshape(-1) for r in rows)
    return out, tgrad, gin, cw.T, cb, decay, bias, skip, ng, gg, gout.reshape(2 * R, D)


def solution(mesh):
    rows, own = P(AXES, None), P(AXES)
    toks = P("dp", "seq", None)
    return jax.shard_map(
        body, mesh=mesh,
        in_specs=(toks, P("dp"), rows, rows, own, P(), P(), P(), own, own, rows, toks),
        out_specs=(toks, toks, rows, rows, own, P(), P(), P(), own, own, rows),
        check_vma=False,
    )
```

time: 1630 us -> 368 us (0.23)
  waiting for transfers between devices: 804 us -> 0 us
  Pallas kernels: 0 us -> 360 us
  matrix products: 355 us -> 0 us
  other arithmetic: 169 us -> 0 us
  blocking collectives: 145 us -> 0 us
  local copies, waits for them, and re-layouts: 117 us -> 6.53 us
    reduce_scatter x2 -> x0, waiting for transfers between devices: 581 us -> none  [the longest x1 373 us: body(): lax.psum_scatter(weight_totals[0], ('dp', 'seq'), scatter_dimension=0, ti...]
    pallas_call x0 -> x3, Pallas kernels: none -> 360 us  [the longest x1 186 us: backward(): pl.pallas_call(functools.partial(backward_kernel, S, PL, RLAG, ZLAG), out...]
    dot_general x38 -> x0, matrix products: 355 us -> none  [the longest x8 133 us: inner_block(): jnp.einsum('ijh,ij,jhp->ihp', fades, intersection, scaled, precision=high...]
    all_gather x6 -> x0, waiting for transfers between devices: 169 us -> none  [the longest x2 64.3 us: entering_2(): everything = jax.tree.map(lambda part: lax.all_gather(part, axis), x)]
    all_gather x5 -> x0, blocking collectives: 105 us -> none  [the longest x1 63.6 us: body(): lax.all_gather(shards[1], ('dp', 'seq'), axis=0, tiled=True)]
    unnamed x10 -> x0, waiting for transfers between devices: 54.3 us -> none
    reduce_sum x15 -> x0, other arithmetic: 47 us -> none  [the longest x2 19.1 us: conv_section(): conv_weight[:, offset] * extended[:, offset:offset + segment, :]]
    unnamed x1 -> x0, blocking collectives: 40 us -> none
  transfers between devices with their start and end apart: 13 -> 0, of which waited for: 7 -> 0; matrix products, arithmetic and copies ran while one was open for 23% -> 0% of each run, Pallas kernels for 0% -> 0%
where the time goes in v1:
time: 368 us; the launch traced here: 367 us
  Pallas kernels  360 us (98%)
  local copies, waits for them, and re-layouts  6.53 us (2%)
    pallas_call x1, Pallas kernels, backward(): pl.pallas_call(functools.partial(backward_kernel, S, PL, RLAG, ZLAG), out...  186 us
    pallas_call x1, Pallas kernels, forward(): pl.pallas_call(functools.partial(forward_kernel, S, PL), out_shape=[sds((...  172 us

profile of v1, /device:TPU:24, one launch (start us, length us, event | category | flops | bytes accessed | tf_op | source)
XLA Modules:
  0.0 367.4 jit_solution(269675945680582535)
XLA Ops:
  0.6 172.0 %forward.1 = (bf16[2,256,1536]{2,1,0:T(8,128)(2,1)}, bf16[17,1536,384]{2,1,0:T(8,128)(2,1)}, bf16[4,512,384]{2,1,0:T(8,128)(2,1)}, bf16[9,2,272,384]{3,2,1,0:T(8...) custom-call(s32[2]{0:T(128)} %lengths.3, ...), custom_call_target="tpu_custom_call" | custom-call | tf_op jit(solution)/shard_map/forward/pallas_call | solution.py:645
  172.6 185.6 %backward.1 = (bf16[2,256,1536]{2,1,0:T(8,128)(2,1)}, f32[8,128]{1,0:T(8,128)}, f32[48,6528]{1,0:T(8,128)}, f32[2,48,1536]{2,1,0:T(8,128)}, f32[8,128]{1,0:T(8,128)}) custom-call(s32[2]{0:T(128)} %lengths.3, f32[1,48]{1,0:T(1,128)} %bitcast.18, f32[1,48]{1,0:T(1,128)} %bitcast.20, f32[1,48]{1,0:T(1,128)} %bitcast.22, f32[8,1536]{1,0:T(8,128)} %get-tuple-element.48.ngain, ...), custom_call_target="tpu_custom_call" | custom-call | tf_op jit(solution)/shard_map/backward/pallas_call | solution.py:1300
  358.2 0.0 copy-start
  358.3 1.4 copy-done
  359.7 0.0 copy-start.1
  359.7 1.4 copy-done.1
  361.1 0.0 copy-start.2
  361.1 1.3 copy-done.2
  362.4 0.0 copy-start.3
  362.4 1.1 copy-done.3
  363.4 0.0 copy-start.4
  363.4 0.7 copy-done.4
  364.1 0.0 copy-start.5
  364.1 0.7 copy-done.5
  364.8 2.6 deliver.1
Async XLA Ops:
  358.2 1.4 copy-start
  359.7 1.4 copy-start.1
  361.1 1.3 copy-start.2
  362.4 1.1 copy-start.3
  363.4 0.7 copy-start.4
  364.1 0.7 copy-start.5

commit v2 on v1

--- a/solution.py
+++ b/solution.py
@@ -19,8 +19,9 @@
 GH = CW // HDIM
 NI = 1 + 2 * GROUPS
 NO = D // CW
+EARLY = 2
 MID = 2 + GROUPS
-GATE = MID + NO // 2
+GATE = MID + EARLY
 LATE = GATE + GROUPS
 HALO = 16
 EPS = 1e-05
@@ -30,7 +31,7 @@
 bf16 = jnp.bfloat16
 AXES = ("dp", "seq")
 LAG = 2
-AHEAD = 4
+SLACK = 1
 
 
 def flip(p, w):
@@ -106,11 +107,25 @@
                 def _():
                     f(fn(k), R, land and land(k))
 
-    def zcopy(self, ref, R, land, k, o, recv=False):
+    def zcopy(self, ref, R, land, k, way, h):
         at = self.at
-        src = at.behind(o) if recv else at.z
+        src = at.z - h if way == 0 else at.z + h
         blk = ref.at[pl.ds((at.d * at.S + src) * R, R)] if land is None else land.at[src]
-        return remote(blk, blk, self.zs.at[k, o - 1], self.zr.at[k, o - 1], at.along(o))
+        to = (at.d, at.z + 1 if way == 0 else at.z - 1)
+        n = min(h, at.S - 2)
+        return remote(blk, blk, self.zs.at[k, way, n], self.zr.at[k, way, n], to)
+
+    def zarrival(self, ref, R, land, k, way, h):
+        at = self.at
+        src = at.z - h if way == 0 else at.z + h
+        blk = ref.at[pl.ds((at.d * at.S + src) * R, R)] if land is None else land.at[src]
+        return remote(blk, blk, self.zs.at[k, way, 0], self.zr.at[k, way, h - 1], at.along(1))
+
+    def holds(self, way, h):
+        return self.at.z >= h if way == 0 else self.at.z + h < self.at.S
+
+    def goes_on(self, way):
+        return self.at.z < self.at.S - 1 if way == 0 else self.at.z > 0
 
     def half(self, ref, R, q, c, h):
         n = self.at.S * R // 2
@@ -133,16 +148,23 @@
 
     def send_z(self, k):
         def f(ref, R, land):
-            for o in range(1, self.at.S):
-                self.zcopy(ref, R, land, k, o).start()
+            for way in range(2):
+                pl.when(self.goes_on(way))(lambda: self.zcopy(ref, R, land, k, way, 0).start())
+
+        self.each(k, f)
+
+    def hop(self, k, h):
+        def f(ref, R, land):
+            for way in range(2):
+                pl.when(self.holds(way, h))(lambda: self.zarrival(ref, R, land, k, way, h).wait_recv())
+                if h < self.at.S - 1:
+                    pl.when(self.holds(way, h) & self.goes_on(way))(lambda: self.zcopy(ref, R, land, k, way, h).start())
 
         self.each(k, f)
 
     def stage(self, k, j):
         def f(ref, R, land):
             if j == 0:
-                for o in range(1, self.at.S):
-                    self.zcopy(ref, R, land, k, o, True).wait_recv()
                 if land is not None:
                     rows = self.at.S * R
                     own = ref.at[pl.ds(pl.multiple_of(self.at.d * rows, 16), rows)]
@@ -171,8 +193,10 @@
 
     def sent(self, k):
         def f(ref, R, land):
-            for o in range(1, self.at.S):
-                self.zcopy(ref, R, land, k, o).wait_send()
+            for way in range(2):
+                for h in range(self.at.S - 1):
+                    pl.when(self.holds(way, h) & self.goes_on(way))(
+                        lambda: self.zcopy(ref, R, land, k, way, h).wait_send())
             for h in range(2):
                 for j in range(self.at.m):
                     for i in range(2**j):
@@ -288,7 +312,7 @@
         return ((k >= MID) & (k < GATE)) | ((k >= LATE) & (k < n))
 
     def chunk_i(k):
-        return k - 1 - (NO // 2) * lax.div(k, GATE)
+        return k - 1 - EARLY * lax.div(k, GATE)
 
     def chunk_o(k):
         return k - MID - GROUPS * lax.div(k, LATE)
@@ -320,8 +344,6 @@
     at.barrier()
     for c in range(NO):
         local(c).wait()
-    for k in range(AHEAD):
-        ga.send_z(k)
 
     def halo_copy():
         return remote(tok.at[:, pl.ds(T - HALO, HALO)], halo, hsem.at[0], hsem.at[1], at.along(1))
@@ -441,12 +463,12 @@
                 xs = jnp.concatenate([hi[:, sl], lo[:, sl]], axis=1)
                 top, bot = [], []
                 for h in (2 * q, 2 * q + 1):
-                    mt = (gram[s, :H, :H] * fade(ldc, ldr, h, 0, H, H)).astype(bf16)
-                    mb = (gram[s, H:, :] * fade(ldc, ldr, h, H, H, T)).astype(bf16)
+                    mt, mt_low = halves(gram[s, :H, :H] * fade(ldc, ldr, h, 0, H, H))
+                    mb, mb_low = halves(gram[s, H:, :] * fade(ldc, ldr, h, H, H, T))
                     r = dot(mt, xs[:H])
-                    top.append(r[:, :128] + r[:, 128:])
+                    top.append(r[:, :128] + r[:, 128:] + dot(mt_low, xs[:H, :128]))
                     r = dot(mb, xs)
-                    bot.append(r[:, :128] + r[:, 128:])
+                    bot.append(r[:, :128] + r[:, 128:] + dot(mb_low, xs[:, :128]))
                 ybuf[g, s, :H, sl] = jnp.where(low, top[0], top[1]) + skip[:, sl] * V[:H, sl]
                 ybuf[g, s, H:, sl] = jnp.where(low, bot[0], bot[1]) + skip[:, sl] * V[H:, sl]
             return carry
@@ -525,9 +547,10 @@
             normed[s, 0:T] = (live(s) * normed[s, 0:T].astype(f32)).astype(bf16)
 
     def out_chunk(c, carry):
-        branch = dot(nyb[0], wo[c, :CW])
-        for g in range(1, GROUPS):
-            branch = branch + dot(nyb[g], wo[c, g * CW : (g + 1) * CW])
+        branch = jnp.zeros((rows, CW), f32)
+        for g in range(0, GROUPS, 2):
+            two = jnp.concatenate([nyb[g], nyb[g + 1]], axis=1)
+            branch = branch + dot(two, wo[c, g * CW : (g + 2) * CW])
         branch = branch.reshape(seqs, T, CW)
         lane = pl.ds(pl.multiple_of(c * CW, 128), CW)
         masked = normed[:, 0:T, lane].reshape(rows, CW)
@@ -535,11 +558,14 @@
             out[s, :, lane] = (tok[s, :, lane].astype(f32) + live(s) * branch[s]).astype(bf16)
 
         def upstream(g, carry):
-            part = wo[c, pl.ds(pl.multiple_of(g * CW, 16), CW)]
-            ybuf[g] += dot(masked, part, NT).reshape(seqs, T, CW)
+            part = wo[c, pl.ds(pl.multiple_of(g * 2 * CW, 16), 2 * CW)]
+            for s in range(seqs):
+                both = dot(masked[s * T : (s + 1) * T], part, NT)
+                ybuf[2 * g, s] += both[:, :CW]
+                ybuf[2 * g + 1, s] += both[:, CW:]
             return carry
 
-        lax.fori_loop(0, GROUPS, upstream, 0)
+        lax.fori_loop(0, GROUPS // 2, upstream, 0)
 
         @pl.when(c == NO - 1)
         def _():
@@ -562,11 +588,13 @@
         def _():
             f(wi.at[chunk_i(k)], owin.at[chunk_i(k)])
 
-    HOP = 3 if S <= 4 else 1
+    HOP = (GATE - 3) // (S - 1)
     last = at.m * LAG + 1
 
     def tick(t, carry):
-        ga.send_z(t + AHEAD)
+        ga.send_z(t + S + SLACK)
+        for h in range(1, S):
+            ga.hop(t + S - h, h)
         for j in range(at.m + 1):
             ga.stage(t - j * LAG, j)
         k = t - last
@@ -575,19 +603,19 @@
         pl.when(k == 0)(unpack)
         pl.when(k == 1)(first_chunk)
         pl.when((k >= 2) & (k < MID))(lambda: values_chunk(k - 2, k - 1))
-        g = k - 3 - HOP * at.z
+        g = k - 3 - HOP * at.z - lax.div(at.z, S - 1) * (GATE - 3 - HOP * (S - 1))
         pl.when((g >= 0) & (g < GROUPS))(lambda: pass_state(g))
         pl.when((k >= GATE) & (k < LATE))(lambda: gate_chunk(k - GATE, k - GATE + 1 + GROUPS))
 
         pl.when(k == LATE)(normalise)
-        late = jnp.clip(k - LATE, -1, NO - NO // 2 - 1)
-        begin = jnp.where(late > 0, late + NO // 2, 0)
-        end = jnp.where(late >= 0, late + NO // 2 + 1, 0)
+        late = jnp.clip(k - LATE, -1, NO - EARLY - 1)
+        begin = jnp.where(late > 0, late + EARLY, 0)
+        end = jnp.where(late >= 0, late + EARLY + 1, 0)
         lax.fori_loop(begin, end, out_chunk, 0)
 
         return carry
 
-    lax.fori_loop(0, n + last, tick, 0)
+    lax.fori_loop(-S - SLACK, n + last, tick, 0)
 
     def finish(k, carry):
         ga.sent(k)
@@ -667,7 +695,7 @@
             V((seqs, T, 128), f32), V((seqs, T, 128), f32), V((8, 128), f32), V((2, seqs, HALO + T, CW), bf16),
             V((2, seqs, T, CW), f32), V((2, T, CW), f32),
             dma((NO,)), dma((n,)), dma((2,)), dma((2, GROUPS)), dma((2,)), dma((2,)), dma((2,)), dma((seqs + 11,)), dma((D // CW, seqs)), dma((1,)),
-            dma((n, S - 1)), dma((n, S - 1)), dma((n, 2 * PL - 2)), dma((n, 2 * PL - 2)), dma((n, 2 * PL)), dma((n, 2 * PL)),
+            dma((n, 2, S - 1)), dma((n, 2, S - 1)), dma((n, 2 * PL - 2)), dma((n, 2 * PL - 2)), dma((n, 2 * PL)), dma((n, 2 * PL)),
         ],
         name="forward",
         compiler_params=pltpu.CompilerParams(collective_id=0, has_side_effects=True, vmem_limit_bytes=63 << 20),
@@ -1017,12 +1045,14 @@
             for h in (2 * q, 2 * q + 1):
                 ft = fade(ldc, ldr, h, 0, H, H)
                 fb = fade(ldc, ldr, h, H, H, T)
-                mt = (gram[s, :H, :H] * ft).astype(bf16)
-                mb = (gram[s, H:, :] * fb).astype(bf16)
+                mt, mt_low = halves(gram[s, :H, :H] * ft)
+                mb, mb_low = halves(gram[s, H:, :] * fb)
                 r0 = dot(jnp.concatenate([mt, mb[:, :H]], axis=0), dyp, TN)
                 r1 = dot(mb[:, H:], dyp[H:], TN)
                 r = jnp.concatenate([r0, r1], axis=0)
-                two.append(r[:, :128] + r[:, 128:])
+                low0 = dot(jnp.concatenate([mt_low, mb_low[:, :H]], axis=0), dyp[:, :128], TN)
+                low1 = dot(mb_low[:, H:], dyp[H:, :128], TN)
+                two.append(r[:, :128] + r[:, 128:] + jnp.concatenate([low0, low1], axis=0))
                 mine = low if h == 2 * q else jnp.logical_not(low)
                 dyh = jnp.concatenate(halves(jnp.where(mine, dY, 0.0)), axis=1)
                 dgt = dgt + ft * dot(dyh[:H], x2[:H], NT)
@@ -1243,8 +1273,9 @@
             lax.fori_loop(2 * t - GROUPS, 2 * t - GROUPS + 2, both, 0)
 
         step = t - 1 - HOP * (S - 1 - at.z)
-        passed = lax.div(2 * step + 2, 3)
-        pl.when((step >= 0) & (lax.rem(step, 3) < 2) & (passed < GROUPS))(lambda: pass_state(passed))
+        passed = lax.div(4 * step + 6, 7)
+        new = passed * 7 < 4 * step + 4
+        pl.when((step >= 0) & new & (passed < GROUPS))(lambda: pass_state(passed))
         def parts_before(t):
             return lax.div(jnp.clip(t - TB, 0, NQ - 2 - TB) * seqs * GROUPS + NQ - 3 - TB, NQ - 2 - TB)
 

time: 368 us -> 364 us (0.989)
  Pallas kernels: 360 us -> 356 us
    pallas_call x1, Pallas kernels: 186 us -> 180 us  [backward(): pl.pallas_call(functools.partial(backward_kernel, S, PL, RLAG, ZLAG), out...]
where the time goes in v2:
time: 364 us; the launch traced here: 363 us
  Pallas kernels  356 us (98%)
  local copies, waits for them, and re-layouts  6.53 us (2%)
    pallas_call x1, Pallas kernels, backward(): pl.pallas_call(functools.partial(backward_kernel, S, PL, RLAG, ZLAG), out...  180 us
    pallas_call x1, Pallas kernels, forward(): pl.pallas_call(functools.partial(forward_kernel, S, PL), out_shape=[sds((...  173 us

profile of v2, /device:TPU:24, one launch (start us, length us, event | category | flops | bytes accessed | tf_op | source)
XLA Modules:
  0.0 362.9 jit_solution(6128486471822507359)
XLA Ops:
  0.6 173.4 %forward.1 = (bf16[2,256,1536]{2,1,0:T(8,128)(2,1)}, bf16[17,1536,384]{2,1,0:T(8,128)(2,1)}, bf16[4,512,384]{2,1,0:T(8,128)(2,1)}, bf16[9,2,272,384]{3,2,1,0:T(8...) custom-call(s32[2]{0:T(128)} %lengths.3, ...), custom_call_target="tpu_custom_call" | custom-call | tf_op jit(solution)/shard_map/forward/pallas_call | solution.py:673
  174.1 179.6 %backward.1 = (bf16[2,256,1536]{2,1,0:T(8,128)(2,1)}, f32[8,128]{1,0:T(8,128)}, f32[48,6528]{1,0:T(8,128)}, f32[2,48,1536]{2,1,0:T(8,128)}, f32[8,128]{1,0:T(8,128)}) custom-call(s32[2]{0:T(128)} %lengths.3, f32[1,48]{1,0:T(1,128)} %bitcast.18, f32[1,48]{1,0:T(1,128)} %bitcast.20, f32[1,48]{1,0:T(1,128)} %bitcast.22, f32[8,1536]{1,0:T(8,128)} %get-tuple-element.48.ngain, ...), custom_call_target="tpu_custom_call" | custom-call | tf_op jit(solution)/shard_map/backward/pallas_call | solution.py:1331
  353.7 0.0 copy-start
  353.7 1.4 copy-done
  355.1 0.0 copy-start.1
  355.1 1.4 copy-done.1
  356.5 0.0 copy-start.2
  356.5 1.3 copy-done.2
  357.8 0.0 copy-start.3
  357.8 1.1 copy-done.3
  358.9 0.0 copy-start.4
  358.9 0.7 copy-done.4
  359.6 0.0 copy-start.5
  359.6 0.7 copy-done.5
  360.3 2.6 deliver.1
Async XLA Ops:
  353.7 1.4 copy-start
  355.1 1.4 copy-start.1
  356.5 1.3 copy-start.2
  357.8 1.1 copy-start.3
  358.9 0.7 copy-start.4
  359.6 0.7 copy-start.5

commit v3 on v2

--- a/solution.py
+++ b/solution.py
@@ -563,13 +563,18 @@
                 both = dot(masked[s * T : (s + 1) * T], part, NT)
                 ybuf[2 * g, s] += both[:, :CW]
                 ybuf[2 * g + 1, s] += both[:, CW:]
+
+            @pl.when(c == NO - 1)
+            def _():
+                two = pl.ds(2 * g, 2)
+                pltpu.make_async_copy(ybuf.at[two], odny.at[two], esem.at[0]).start()
+
             return carry
 
         lax.fori_loop(0, GROUPS // 2, upstream, 0)
 
         @pl.when(c == NO - 1)
         def _():
-            pltpu.make_async_copy(ybuf, odny, esem.at[0]).start()
             for s in range(seqs):
                 t = jnp.zeros((T, 1), f32)
                 for g in range(GROUPS):

time: 364 us -> 364 us (level)
  no operation moved by 1% of the time
where the time goes in v3:
time: 364 us; the launch traced here: 363 us
  Pallas kernels  356 us (98%)
  local copies, waits for them, and re-layouts  6.53 us (2%)
    pallas_call x1, Pallas kernels, backward(): pl.pallas_call(functools.partial(backward_kernel, S, PL, RLAG, ZLAG), out...  180 us
    pallas_call x1, Pallas kernels, forward(): pl.pallas_call(functools.partial(forward_kernel, S, PL), out_shape=[sds((...  173 us

profile of v3, /device:TPU:24, one launch (start us, length us, event | category | flops | bytes accessed | tf_op | source)
XLA Modules:
  0.0 362.8 jit_solution(15057167543754316704)
XLA Ops:
  0.6 173.3 %forward.1 = (bf16[2,256,1536]{2,1,0:T(8,128)(2,1)}, bf16[17,1536,384]{2,1,0:T(8,128)(2,1)}, bf16[4,512,384]{2,1,0:T(8,128)(2,1)}, bf16[9,2,272,384]{3,2,1,0:T(8...) custom-call(s32[2]{0:T(128)} %lengths.3, ...), custom_call_target="tpu_custom_call" | custom-call | tf_op jit(solution)/shard_map/forward/pallas_call | solution.py:678
  174.0 179.6 %backward.1 = (bf16[2,256,1536]{2,1,0:T(8,128)(2,1)}, f32[8,128]{1,0:T(8,128)}, f32[48,6528]{1,0:T(8,128)}, f32[2,48,1536]{2,1,0:T(8,128)}, f32[8,128]{1,0:T(8,128)}) custom-call(s32[2]{0:T(128)} %lengths.3, f32[1,48]{1,0:T(1,128)} %bitcast.18, f32[1,48]{1,0:T(1,128)} %bitcast.20, f32[1,48]{1,0:T(1,128)} %bitcast.22, f32[8,1536]{1,0:T(8,128)} %get-tuple-element.48.ngain, ...), custom_call_target="tpu_custom_call" | custom-call | tf_op jit(solution)/shard_map/backward/pallas_call | solution.py:1336
  353.6 0.0 copy-start
  353.6 1.4 copy-done
  355.0 0.0 copy-start.1
  355.0 1.4 copy-done.1
  356.4 0.0 copy-start.2
  356.4 1.3 copy-done.2
  357.7 0.0 copy-start.3
  357.7 1.1 copy-done.3
  358.8 0.0 copy-start.4
  358.8 0.7 copy-done.4
  359.5 0.0 copy-start.5
  359.5 0.7 copy-done.5
  360.2 2.6 deliver.1
Async XLA Ops:
  353.6 1.4 copy-start
  355.0 1.4 copy-start.1
  356.4 1.3 copy-start.2
  357.7 1.1 copy-start.3
  358.8 0.7 copy-start.4
  359.5 0.7 copy-start.5
